TPU v7x, 32 devices: a whole 2x2x4 slice. The times are simulated.
32 devices in a mesh: groups: 2 (over x), section: 16 (over z, y, core).
Axes of the slice: x: 2, y: 2, z: 4, core: 2. Of those that a mesh axis runs over, the one named last changes fastest.
Arguments:
- hidden_in: bfloat16 [512, 3072], P(('groups', 'section')), parts along dimension 0, may hold values from -0.59765625 to 0.59765625
- latent_in: bfloat16 [512, 64], P(('groups', 'section')), parts along dimension 0, may hold values from -6 to 6
- w_qkv: bfloat16 [3, 3072, 6144], P(None, None, 'section'), may hold values from -0.109375 to 0.109375
- w_out: bfloat16 [6144, 3072], P('section'), may hold values from -0.109375 to 0.109375
- stale_kv: bfloat16 [4, 256, 6144], P('groups', None, 'section'), parts along dimension 0, may hold values from -3 to 3
- qk_gain: float32 [2, 2, 128], replicated, may hold values from 0.6 to 2.4
- block_mod: float32 [4, 3, 3072], P('groups'), parts along dimension 0, may hold values from -4 to 4
- final_mod: float32 [4, 3072], P('groups'), parts along dimension 0, may hold values from -3 to 3
- w_final: bfloat16 [3072, 64], replicated, may hold values from -0.109375 to 0.109375
- w_embed: bfloat16 [64, 3072], replicated, may hold values from -0.75 to 0.75
- patch_flow: int32 [6, 2], replicated, may hold values from 0 to 1, as said below
Outputs:
- hidden_out: bfloat16 [512, 3072], P(('groups', 'section')), parts along dimension 0
- latent_out: bfloat16 [512, 64], P(('groups', 'section')), parts along dimension 0
There are 2 independent parts, one for each index of `groups`. A program takes and returns all parts, laid end to end along the dimension named above; an argument that names none is the same for every part. Nothing has to cross between parts.
Inputs may be any that keep to these rules, and one draw needn't show every extreme that they name: `patch_flow`: each row holds each of 0 to 1 once.
All inputs are finite; a program needn't handle non-finite values.
Results may differ from a plain program's by a relative error of at most 0.03.
Values may be sent and summed in bfloat16 or wider, within the bound.
A program may use at most 128 MiB of HBM per device.

v0:
```python
import math

import jax
import jax.numpy as jnp
from jax import lax
from jax.sharding import PartitionSpec as P

HS = 128
GROUP = 8
TICKS = 6


def for_sending(value):

    def short(part):
        return part.astype(jnp.bfloat16) if part.dtype == jnp.float32 else part

    return jax.tree.map(short, value)


def partner(block, axis, apart):
    count = lax.axis_size(axis)
    route = []
    for low in range(count):
        high = low | 1 << apart
        if high != low and high < count:
            route += [(low, high), (high, low)]
    return lax.ppermute(block, axis, route)


def from_behind(value, axis, by):
    size = lax.axis_size(axis)
    return lax.ppermute(value, axis, [(i, (i + by) % size) for i in range(size)])


def layer_norm(tokens, offset_row, scale_row):
    average = jnp.mean(tokens, axis=-1, keepdims=True)
    centred = tokens - average
    variance = jnp.mean(centred * centred, axis=-1, keepdims=True)
    return (centred * lax.rsqrt(variance + 1e-06) * (1.0 + scale_row) + offset_row).astype(
        jnp.bfloat16
    )


def head_norm(values, gain_row):
    return (
        values * lax.rsqrt(jnp.mean(values * values, axis=-1, keepdims=True) + 1e-06) * gain_row
    ).astype(jnp.bfloat16)


def head_terms_of(
    hidden, w_qkv, w_out, key_cache, value_cache, modulation, norm_gains, patch_index
):
    token_count = hidden.shape[0]
    total_rows = key_cache.shape[0]
    head_count = w_qkv.shape[2] // HS
    normed = layer_norm(hidden.astype(jnp.float32), modulation[0], modulation[1])
    queries = jnp.dot(normed, w_qkv[0], preferred_element_type=jnp.float32).reshape(
        token_count, head_count, HS
    )
    fresh_keys = jnp.dot(normed, w_qkv[1], preferred_element_type=jnp.float32).reshape(
        token_count, head_count, HS
    )
    fresh_values = jnp.dot(normed, w_qkv[2], preferred_element_type=jnp.float32)
    query_norm = head_norm(queries, norm_gains[0])
    key_norm = head_norm(fresh_keys, norm_gains[1]).reshape(token_count, head_count * HS)
    offset = patch_index * token_count
    key_cache = lax.dynamic_update_slice(key_cache, key_norm, (offset, jnp.int32(0)))
    value_cache = lax.dynamic_update_slice(
        value_cache, fresh_values.astype(jnp.bfloat16), (offset, jnp.int32(0))
    )
    scores = jnp.einsum(
        "qhd,khd->hqk",
        query_norm,
        key_cache.reshape(total_rows, head_count, HS),
        preferred_element_type=jnp.float32,
    ) / math.sqrt(HS)
    exp_scores = jnp.exp(scores)
    totals = jnp.sum(exp_scores, axis=-1)
    attended = jnp.einsum(
        "hqk,khd->qhd",
        exp_scores.astype(jnp.bfloat16),
        value_cache.reshape(total_rows, head_count, HS),
        preferred_element_type=jnp.float32,
    )
    attended = (
        (attended / jnp.transpose(totals)[:, :, None])
        .astype(jnp.bfloat16)
        .reshape(token_count, head_count * HS)
    )
    return (jnp.dot(attended, w_out, preferred_element_type=jnp.float32), key_cache, value_cache)


def restart(hidden, latent, final_mod, w_final, w_embed, at_start):
    normed = layer_norm(hidden.astype(jnp.float32), final_mod[0], final_mod[1])
    velocity = jnp.dot(normed, w_final, preferred_element_type=jnp.float32)
    renewed = (latent.astype(jnp.float32) + velocity).astype(jnp.bfloat16)
    embedded = jnp.dot(renewed, w_embed, preferred_element_type=jnp.float32).astype(jnp.bfloat16)
    return (jnp.where(at_start, embedded, hidden), jnp.where(at_start, renewed, latent))


def collect(pieces, position, levels, fetcher):
    for bit_number in range(levels):
        others = fetcher(pieces, bit_number)
        lower_half = position >> bit_number & 1 == 0
        pieces = tuple(
            (
                jnp.where(
                    lower_half,
                    jnp.concatenate([own_piece, other_piece], 0),
                    jnp.concatenate([other_piece, own_piece], 0),
                )
                for own_piece, other_piece in zip(pieces, others)
            )
        )
    return pieces


def body(
    hidden_in,
    latent_in,
    w_qkv,
    w_out,
    stale_kv,
    qk_gain,
    block_mod,
    final_mod,
    w_final,
    w_embed,
    patch_flow,
):
    device_index = lax.axis_index("section")
    section_index = device_index // GROUP
    position = device_index % GROUP
    levels = GROUP.bit_length() - 1
    modulation = lax.dynamic_index_in_dim(block_mod, section_index, 0, keepdims=False)
    norm_gains = lax.dynamic_index_in_dim(qk_gain, section_index, 0, keepdims=False)
    key_cache = stale_kv[0]
    value_cache = stale_kv[1]
    at_start = section_index == 0

    def fetch_rows(payload, bit_number):
        return jax.tree.map(
            lambda part, own: part.astype(own.dtype),
            partner(for_sending(payload), "section", bit_number),
            payload,
        )

    hidden_out, latent_out = (hidden_in, latent_in)
    for tick_index in range(TICKS):
        (hidden,) = collect((hidden_out,), position, levels, fetch_rows)
        patch_index = lax.dynamic_index_in_dim(
            patch_flow[tick_index], section_index, 0, keepdims=False
        )
        partial_value, key_cache, value_cache = head_terms_of(
            hidden, w_qkv, w_out, key_cache, value_cache, modulation, norm_gains, patch_index
        )
        for bit_number in reversed(range(levels)):
            half_rows = partial_value.shape[0] // 2
            lower_half = position >> bit_number & 1 == 0
            kept_part = jnp.where(lower_half, partial_value[:half_rows], partial_value[half_rows:])
            sent_part = jnp.where(lower_half, partial_value[half_rows:], partial_value[:half_rows])
            partial_value = kept_part + partner(
                sent_part.astype(jnp.bfloat16), "section", bit_number
            ).astype(sent_part.dtype)
        result = (hidden_out.astype(jnp.float32) + modulation[2] * partial_value).astype(
            jnp.bfloat16
        )
        hidden_out, latent_out = from_behind((result, latent_out), "section", GROUP)
        hidden_out, latent_out = restart(
            hidden_out, latent_out, final_mod, w_final, w_embed, at_start
        )
    return (hidden_out, latent_out)


def solution(mesh):
    in_specs = (
        P(("groups", "section"), None),
        P(("groups", "section"), None),
        P(None, None, "section"),
        P("section", None),
        P("groups", None, "section"),
        P(),
        P("groups", None, None),
        P("groups", None),
        P(),
        P(),
        P(),
    )
    out_specs = (P(("groups", "section"), None), P(("groups", "section"), None))
    return jax.shard_map(body, mesh=mesh, in_specs=in_specs, out_specs=out_specs, check_vma=False)
```

profile of v0, /device:TPU:0, one launch (start us, length us, event | category | flops | bytes accessed | tf_op | source)
XLA Modules:
  0.0 390.2 jit_solution(14024831218794991269)
XLA Ops:
  1.2 5.2 %slice_bitcast_fusion.1 = (bf16[384,3072]{0,1:T(8,128)(2,1)}, bf16[384,3072]{0,1:T(8,128)(2,1)}) fusion(bf16[3,3072,384]{2,1,0:T(8,128)(2,1)} %param.13), kind=kLoop, calls=%fused_computation.25 | loop fusion | bytes 9437184 | tf_op jit(solution)/shard_map/dot_general | solution.py:58
  6.5 2.6 collective-permute-start.2
  9.8 4.7 %collective-permute-done.2 = bf16[32,3072]{1,0:T(8,128)(2,1)S(1)} collective-permute-done((bf16[32,3072]{1,0:T(8,128)(2,1)S(1)}, bf16[32,3072]{1,0:T(8,128)(2,1)S(1)}, u32[]{:S(2)}, u32[]{:S(2)}) %collective-permute-start.2) | collective-permute-done | bytes 196640 | tf_op jit(solution)/shard_map/ppermute | solution.py:28
  17.0 4.3 %copy.41 = bf16[384,3072]{1,0:T(8,128)(2,1)} copy(bf16[384,3072]{0,1:T(8,128)(2,1)} %get-tuple-element.2) | data formatting | bytes 4718592 | tf_op jit(solution)/shard_map/dot_general | solution.py:58
  21.3 4.3 %copy.43 = bf16[384,3072]{1,0:T(8,128)(2,1)} copy(bf16[384,3072]{0,1:T(8,128)(2,1)} %get-tuple-element.3) | data formatting | bytes 4718592 | tf_op jit(solution)/shard_map/dot_general | solution.py:61
  30.6 3.3 multiply_reduce_fusion.11
  36.9 2.7 multiply_reduce_fusion.10
  41.5 10.1 %collective-permute-done.4 = bf16[64,3072]{1,0:T(8,128)(2,1)S(1)} collective-permute-done((bf16[64,3072]{1,0:T(8,128)(2,1)S(1)}, bf16[64,3072]{1,0:T(8,128)(2,1)S(1)}, u32[]{:S(2)}, u32[]{:S(2)}) %collective-permute-start.4) | collective-permute-done | bytes 393248 | tf_op jit(solution)/shard_map/ppermute | solution.py:28
  53.3 4.2 %collective-permute-done.5 = bf16[32,3072]{1,0:T(8,128)(2,1)S(1)} collective-permute-done((bf16[32,3072]{1,0:T(8,128)(2,1)S(1)}, bf16[32,3072]{1,0:T(8,128)(2,1)S(1)}, u32[]{:S(2)}, u32[]{:S(2)}) %collective-permute-start.5) | collective-permute-done | bytes 196640 | tf_op jit(solution)/shard_map/ppermute | solution.py:28
  57.7 2.6 collective-permute-start
  61.7 6.5 %collective-permute-done.7 = bf16[16,3072]{1,0:T(8,128)(2,1)S(1)} collective-permute-done((bf16[16,3072]{1,0:T(8,128)(2,1)S(1)}, bf16[16,3072]{1,0:T(8,128)(2,1)S(1)}, u32[]{:S(2)}, u32[]{:S(2)}) %collective-permute-start.7) | collective-permute-done | bytes 98336 | tf_op jit(solution)/shard_map/ppermute | solution.py:33
  73.6 5.4 %collective-permute-done.10 = bf16[32,3072]{1,0:T(8,128)(2,1)S(1)} collective-permute-done((bf16[32,3072]{1,0:T(8,128)(2,1)S(1)}, bf16[32,3072]{1,0:T(8,128)(2,1)S(1)}, u32[]{:S(2)}, u32[]{:S(2)}) %collective-permute-start.10) | collective-permute-done | bytes 196640 | tf_op jit(solution)/shard_map/ppermute | solution.py:28
  81.3 8.3 %collective-permute-done.11 = bf16[64,3072]{1,0:T(8,128)(2,1)} collective-permute-done((bf16[64,3072]{1,0:T(8,128)(2,1)S(1)}, bf16[64,3072]{1,0:T(8,128)(2,1)}, u32[]{:S(2)}, u32[]{:S(2)}) %collective-permute-start.11) | collective-permute-done | bytes 393248 | tf_op jit(solution)/shard_map/ppermute | solution.py:28
  92.6 3.7 multiply_reduce_fusion.9
  96.8 2.8 multiply_reduce_fusion.8
  108.2 9.1 %collective-permute-done.12 = bf16[64,3072]{1,0:T(8,128)(2,1)S(1)} collective-permute-done((bf16[64,3072]{1,0:T(8,128)(2,1)S(1)}, bf16[64,3072]{1,0:T(8,128)(2,1)S(1)}, u32[]{:S(2)}, u32[]{:S(2)}) %collective-permute-start.12) | collective-permute-done | bytes 393248 | tf_op jit(solution)/shard_map/ppermute | solution.py:28
  119.1 4.2 %collective-permute-done.13 = bf16[32,3072]{1,0:T(8,128)(2,1)S(1)} collective-permute-done((bf16[32,3072]{1,0:T(8,128)(2,1)S(1)}, bf16[32,3072]{1,0:T(8,128)(2,1)S(1)}, u32[]{:S(2)}, u32[]{:S(2)}) %collective-permute-start.13) | collective-permute-done | bytes 196640 | tf_op jit(solution)/shard_map/ppermute | solution.py:28
  127.8 5.1 %collective-permute-done.15 = bf16[16,3072]{1,0:T(8,128)(2,1)S(1)} collective-permute-done((bf16[16,3072]{1,0:T(8,128)(2,1)S(1)}, bf16[16,3072]{1,0:T(8,128)(2,1)S(1)}, u32[]{:S(2)}, u32[]{:S(2)}) %collective-permute-start.15) | collective-permute-done | bytes 98336 | tf_op jit(solution)/shard_map/ppermute | solution.py:33
  137.3 5.4 %collective-permute-done.18 = bf16[32,3072]{1,0:T(8,128)(2,1)S(1)} collective-permute-done((bf16[32,3072]{1,0:T(8,128)(2,1)S(1)}, bf16[32,3072]{1,0:T(8,128)(2,1)S(1)}, u32[]{:S(2)}, u32[]{:S(2)}) %collective-permute-start.18) | collective-permute-done | bytes 196640 | tf_op jit(solution)/shard_map/ppermute | solution.py:28
  145.3 8.0 %collective-permute-done.19 = bf16[64,3072]{1,0:T(8,128)(2,1)} collective-permute-done((bf16[64,3072]{1,0:T(8,128)(2,1)S(1)}, bf16[64,3072]{1,0:T(8,128)(2,1)}, u32[]{:S(2)}, u32[]{:S(2)}) %collective-permute-start.19) | collective-permute-done | bytes 393248 | tf_op jit(solution)/shard_map/ppermute | solution.py:28
  156.3 3.8 multiply_reduce_fusion.7
  160.7 2.8 multiply_reduce_fusion.6
  172.1 9.1 %collective-permute-done.20 = bf16[64,3072]{1,0:T(8,128)(2,1)S(1)} collective-permute-done((bf16[64,3072]{1,0:T(8,128)(2,1)S(1)}, bf16[64,3072]{1,0:T(8,128)(2,1)S(1)}, u32[]{:S(2)}, u32[]{:S(2)}) %collective-permute-start.20) | collective-permute-done | bytes 393248 | tf_op jit(solution)/shard_map/ppermute | solution.py:28
  183.0 4.2 %collective-permute-done.21 = bf16[32,3072]{1,0:T(8,128)(2,1)S(1)} collective-permute-done((bf16[32,3072]{1,0:T(8,128)(2,1)S(1)}, bf16[32,3072]{1,0:T(8,128)(2,1)S(1)}, u32[]{:S(2)}, u32[]{:S(2)}) %collective-permute-start.21) | collective-permute-done | bytes 196640 | tf_op jit(solution)/shard_map/ppermute | solution.py:28
  191.7 5.1 %collective-permute-done.23 = bf16[16,3072]{1,0:T(8,128)(2,1)S(1)} collective-permute-done((bf16[16,3072]{1,0:T(8,128)(2,1)S(1)}, bf16[16,3072]{1,0:T(8,128)(2,1)S(1)}, u32[]{:S(2)}, u32[]{:S(2)}) %collective-permute-start.23) | collective-permute-done | bytes 98336 | tf_op jit(solution)/shard_map/ppermute | solution.py:33
  201.2 5.4 %collective-permute-done.26 = bf16[32,3072]{1,0:T(8,128)(2,1)S(1)} collective-permute-done((bf16[32,3072]{1,0:T(8,128)(2,1)S(1)}, bf16[32,3072]{1,0:T(8,128)(2,1)S(1)}, u32[]{:S(2)}, u32[]{:S(2)}) %collective-permute-start.26) | collective-permute-done | bytes 196640 | tf_op jit(solution)/shard_map/ppermute | solution.py:28
  209.5 7.8 %collective-permute-done.27 = bf16[64,3072]{1,0:T(8,128)(2,1)} collective-permute-done((bf16[64,3072]{1,0:T(8,128)(2,1)S(1)}, bf16[64,3072]{1,0:T(8,128)(2,1)}, u32[]{:S(2)}, u32[]{:S(2)}) %collective-permute-start.27) | collective-permute-done | bytes 393248 | tf_op jit(solution)/shard_map/ppermute | solution.py:28
  220.2 3.6 multiply_reduce_fusion.5
  224.4 2.8 multiply_reduce_fusion.4
  227.8 2.6 fusion.81
  235.8 9.1 %collective-permute-done.28 = bf16[64,3072]{1,0:T(8,128)(2,1)S(1)} collective-permute-done((bf16[64,3072]{1,0:T(8,128)(2,1)S(1)}, bf16[64,3072]{1,0:T(8,128)(2,1)S(1)}, u32[]{:S(2)}, u32[]{:S(2)}) %collective-permute-start.28) | collective-permute-done | bytes 393248 | tf_op jit(solution)/shard_map/ppermute | solution.py:28
  246.7 4.2 %collective-permute-done.29 = bf16[32,3072]{1,0:T(8,128)(2,1)S(1)} collective-permute-done((bf16[32,3072]{1,0:T(8,128)(2,1)S(1)}, bf16[32,3072]{1,0:T(8,128)(2,1)S(1)}, u32[]{:S(2)}, u32[]{:S(2)}) %collective-permute-start.29) | collective-permute-done | bytes 196640 | tf_op jit(solution)/shard_map/ppermute | solution.py:28
  255.4 5.1 %collective-permute-done.31 = bf16[16,3072]{1,0:T(8,128)(2,1)S(1)} collective-permute-done((bf16[16,3072]{1,0:T(8,128)(2,1)S(1)}, bf16[16,3072]{1,0:T(8,128)(2,1)S(1)}, u32[]{:S(2)}, u32[]{:S(2)}) %collective-permute-start.31) | collective-permute-done | bytes 98336 | tf_op jit(solution)/shard_map/ppermute | solution.py:33
  264.9 5.4 %collective-permute-done.34 = bf16[32,3072]{1,0:T(8,128)(2,1)S(1)} collective-permute-done((bf16[32,3072]{1,0:T(8,128)(2,1)S(1)}, bf16[32,3072]{1,0:T(8,128)(2,1)S(1)}, u32[]{:S(2)}, u32[]{:S(2)}) %collective-permute-start.34) | collective-permute-done | bytes 196640 | tf_op jit(solution)/shard_map/ppermute | solution.py:28
  272.7 8.2 %collective-permute-done.35 = bf16[64,3072]{1,0:T(8,128)(2,1)} collective-permute-done((bf16[64,3072]{1,0:T(8,128)(2,1)S(1)}, bf16[64,3072]{1,0:T(8,128)(2,1)}, u32[]{:S(2)}, u32[]{:S(2)}) %collective-permute-start.35) | collective-permute-done | bytes 393248 | tf_op jit(solution)/shard_map/ppermute | solution.py:28
  283.9 3.6 multiply_reduce_fusion.3
  288.1 3.0 multiply_reduce_fusion.2
  291.8 2.6 fusion.84
  299.8 9.1 %collective-permute-done.36 = bf16[64,3072]{1,0:T(8,128)(2,1)S(1)} collective-permute-done((bf16[64,3072]{1,0:T(8,128)(2,1)S(1)}, bf16[64,3072]{1,0:T(8,128)(2,1)S(1)}, u32[]{:S(2)}, u32[]{:S(2)}) %collective-permute-start.36) | collective-permute-done | bytes 393248 | tf_op jit(solution)/shard_map/ppermute | solution.py:28
  310.7 4.2 %collective-permute-done.37 = bf16[32,3072]{1,0:T(8,128)(2,1)S(1)} collective-permute-done((bf16[32,3072]{1,0:T(8,128)(2,1)S(1)}, bf16[32,3072]{1,0:T(8,128)(2,1)S(1)}, u32[]{:S(2)}, u32[]{:S(2)}) %collective-permute-start.37) | collective-permute-done | bytes 196640 | tf_op jit(solution)/shard_map/ppermute | solution.py:28
  319.4 5.1 %collective-permute-done.39 = bf16[16,3072]{1,0:T(8,128)(2,1)S(1)} collective-permute-done((bf16[16,3072]{1,0:T(8,128)(2,1)S(1)}, bf16[16,3072]{1,0:T(8,128)(2,1)S(1)}, u32[]{:S(2)}, u32[]{:S(2)}) %collective-permute-start.39) | collective-permute-done | bytes 98336 | tf_op jit(solution)/shard_map/ppermute | solution.py:33
  328.9 5.4 %collective-permute-done.42 = bf16[32,3072]{1,0:T(8,128)(2,1)S(1)} collective-permute-done((bf16[32,3072]{1,0:T(8,128)(2,1)S(1)}, bf16[32,3072]{1,0:T(8,128)(2,1)S(1)}, u32[]{:S(2)}, u32[]{:S(2)}) %collective-permute-start.42) | collective-permute-done | bytes 196640 | tf_op jit(solution)/shard_map/ppermute | solution.py:28
  336.9 8.0 %collective-permute-done.43 = bf16[64,3072]{1,0:T(8,128)(2,1)} collective-permute-done((bf16[64,3072]{1,0:T(8,128)(2,1)S(1)}, bf16[64,3072]{1,0:T(8,128)(2,1)}, u32[]{:S(2)}, u32[]{:S(2)}) %collective-permute-start.43) | collective-permute-done | bytes 393248 | tf_op jit(solution)/shard_map/ppermute | solution.py:28
  347.9 3.6 multiply_reduce_fusion.1
  352.1 2.8 multiply_reduce_fusion
  363.5 9.1 %collective-permute-done.44 = bf16[64,3072]{1,0:T(8,128)(2,1)S(1)} collective-permute-done((bf16[64,3072]{1,0:T(8,128)(2,1)S(1)}, bf16[64,3072]{1,0:T(8,128)(2,1)S(1)}, u32[]{:S(2)}, u32[]{:S(2)}) %collective-permute-start.44) | collective-permute-done | bytes 393248 | tf_op jit(solution)/shard_map/ppermute | solution.py:28
  374.4 4.2 %collective-permute-done.45 = bf16[32,3072]{1,0:T(8,128)(2,1)S(1)} collective-permute-done((bf16[32,3072]{1,0:T(8,128)(2,1)S(1)}, bf16[32,3072]{1,0:T(8,128)(2,1)S(1)}, u32[]{:S(2)}, u32[]{:S(2)}) %collective-permute-start.45) | collective-permute-done | bytes 196640 | tf_op jit(solution)/shard_map/ppermute | solution.py:28
  383.0 5.1 %collective-permute-done.47 = bf16[16,3072]{1,0:T(8,128)(2,1)S(1)} collective-permute-done((bf16[16,3072]{1,0:T(8,128)(2,1)S(1)}, bf16[16,3072]{1,0:T(8,128)(2,1)S(1)}, u32[]{:S(2)}, u32[]{:S(2)}) %collective-permute-start.47) | collective-permute-done | bytes 98336 | tf_op jit(solution)/shard_map/ppermute | solution.py:33
  (384 shorter events, 129.6 us)
Async XLA Ops:
  0.6 5.8 %collective-permute-start.1 = (bf16[16,3072]{1,0:T(8,128)(2,1)}, bf16[16,3072]{1,0:T(8,128)(2,1)S(1)}, u32[]{:S(2)}, u32[]{:S(2)}) collective-permute-start(bf16[16,3072]{1,0:T(8,128)(2,1)} %param.11), channel_id=1, source_target_pairs={{0,1},{1,0},{2,3},{3,2},{4,5},{5,4},{6,7},{7,6},{8,9},{9,8},{10,11... | collective-permute-start | bytes 294920 | tf_op jit(solution)/shard_map/ppermute | solution.py:28
  6.5 8.0 %collective-permute-start.2 = (bf16[32,3072]{1,0:T(8,128)(2,1)S(1)}, bf16[32,3072]{1,0:T(8,128)(2,1)S(1)}, u32[]{:S(2)}, u32[]{:S(2)}) collective-permute-start(bf16[32,3072]{1,0:T(8,128)(2,1)S(1)} %maximum_select_fusion.12), channel_id=1, source_target_pairs={{0,2},{2,0},{1,3},{3,1},{4,6},{6,4},{5,7},{7,5},{8,10},{10,8},{9,1... | collective-permute-start | bytes 589832 | tf_op jit(solution)/shard_map/ppermute | solution.py:28
  14.6 15.3 %collective-permute-start.3 = (bf16[64,3072]{1,0:T(8,128)(2,1)S(1)}, bf16[64,3072]{1,0:T(8,128)(2,1)S(1)}, u32[]{:S(2)}, u32[]{:S(2)}) collective-permute-start(bf16[64,3072]{1,0:T(8,128)(2,1)S(1)} %maximum_select_fusion.6), channel_id=1, source_target_pairs={{0,4},{4,0},{1,5},{5,1},{2,6},{6,2},{3,7},{7,3},{8,12},{12,8},{9,1... | collective-permute-start | bytes 1179656 | tf_op jit(solution)/shard_map/ppermute | solution.py:28
  41.2 10.4 %collective-permute-start.4 = (bf16[64,3072]{1,0:T(8,128)(2,1)S(1)}, bf16[64,3072]{1,0:T(8,128)(2,1)S(1)}, u32[]{:S(2)}, u32[]{:S(2)}) collective-permute-start(bf16[64,3072]{1,0:T(8,128)(2,1)S(1)} %select_convert_fusion.5), channel_id=1, source_target_pairs={{0,4},{4,0},{1,5},{5,1},{2,6},{6,2},{3,7},{7,3},{8,12},{12,8},{9,1... | collective-permute-start | bytes 1179656 | tf_op jit(solution)/shard_map/ppermute | solution.py:28
  51.7 5.7 %collective-permute-start.5 = (bf16[32,3072]{1,0:T(8,128)(2,1)S(1)}, bf16[32,3072]{1,0:T(8,128)(2,1)S(1)}, u32[]{:S(2)}, u32[]{:S(2)}) collective-permute-start(bf16[32,3072]{1,0:T(8,128)(2,1)S(1)} %select_convert_fusion.11), channel_id=1, source_target_pairs={{0,2},{2,0},{1,3},{3,1},{4,6},{6,4},{5,7},{7,5},{8,10},{10,8},{9,1... | collective-permute-start | bytes 589832 | tf_op jit(solution)/shard_map/ppermute | solution.py:28
  57.6 2.7 collective-permute-start.6
  57.7 10.9 %collective-permute-start = (bf16[16,64]{1,0:T(8,128)(2,1)S(1)}, bf16[16,64]{1,0:T(8,128)(2,1)S(1)}, u32[]{:S(2)}, u32[]{:S(2)}) collective-permute-start(bf16[16,64]{1,0:T(8,128)(2,1)S(1)} %copy-done.63), channel_id=1, source_target_pairs={{0,8},{1,9},{2,10},{3,11},{4,12},{5,13},{6,14},{7,15},{8,0},{9,1},... | collective-permute-start | bytes 6152 | tf_op jit(solution)/shard_map/ppermute | solution.py:33
  60.4 7.8 %collective-permute-start.7 = (bf16[16,3072]{1,0:T(8,128)(2,1)S(1)}, bf16[16,3072]{1,0:T(8,128)(2,1)S(1)}, u32[]{:S(2)}, u32[]{:S(2)}) collective-permute-start(bf16[16,3072]{1,0:T(8,128)(2,1)S(1)} %add_convert_fusion.5), channel_id=1, source_target_pairs={{0,8},{1,9},{2,10},{3,11},{4,12},{5,13},{6,14},{7,15},{8,0},{9,1},... | collective-permute-start | bytes 294920 | tf_op jit(solution)/shard_map/ppermute | solution.py:33
  70.6 1.4 collective-permute-start.9
  72.0 7.0 %collective-permute-start.10 = (bf16[32,3072]{1,0:T(8,128)(2,1)S(1)}, bf16[32,3072]{1,0:T(8,128)(2,1)S(1)}, u32[]{:S(2)}, u32[]{:S(2)}) collective-permute-start(bf16[32,3072]{1,0:T(8,128)(2,1)S(1)} %maximum_select_fusion.13), channel_id=1, source_target_pairs={{0,2},{2,0},{1,3},{3,1},{4,6},{6,4},{5,7},{7,5},{8,10},{10,8},{9,1... | collective-permute-start | bytes 589832 | tf_op jit(solution)/shard_map/ppermute | solution.py:28
  79.1 10.5 %collective-permute-start.11 = (bf16[64,3072]{1,0:T(8,128)(2,1)S(1)}, bf16[64,3072]{1,0:T(8,128)(2,1)}, u32[]{:S(2)}, u32[]{:S(2)}) collective-permute-start(bf16[64,3072]{1,0:T(8,128)(2,1)S(1)} %maximum_select_fusion.7), channel_id=1, source_target_pairs={{0,4},{4,0},{1,5},{5,1},{2,6},{6,2},{3,7},{7,3},{8,12},{12,8},{9,1... | collective-permute-start | bytes 1179656 | tf_op jit(solution)/shard_map/ppermute | solution.py:28
  107.9 9.5 %collective-permute-start.12 = (bf16[64,3072]{1,0:T(8,128)(2,1)S(1)}, bf16[64,3072]{1,0:T(8,128)(2,1)S(1)}, u32[]{:S(2)}, u32[]{:S(2)}) collective-permute-start(bf16[64,3072]{1,0:T(8,128)(2,1)S(1)} %select_convert_fusion.4), channel_id=1, source_target_pairs={{0,4},{4,0},{1,5},{5,1},{2,6},{6,2},{3,7},{7,3},{8,12},{12,8},{9,1... | collective-permute-start | bytes 1179656 | tf_op jit(solution)/shard_map/ppermute | solution.py:28
  117.6 5.7 %collective-permute-start.13 = (bf16[32,3072]{1,0:T(8,128)(2,1)S(1)}, bf16[32,3072]{1,0:T(8,128)(2,1)S(1)}, u32[]{:S(2)}, u32[]{:S(2)}) collective-permute-start(bf16[32,3072]{1,0:T(8,128)(2,1)S(1)} %select_convert_fusion.10), channel_id=1, source_target_pairs={{0,2},{2,0},{1,3},{3,1},{4,6},{6,4},{5,7},{7,5},{8,10},{10,8},{9,1... | collective-permute-start | bytes 589832 | tf_op jit(solution)/shard_map/ppermute | solution.py:28
  123.4 1.4 collective-permute-start.14
  124.8 8.1 %collective-permute-start.15 = (bf16[16,3072]{1,0:T(8,128)(2,1)S(1)}, bf16[16,3072]{1,0:T(8,128)(2,1)S(1)}, u32[]{:S(2)}, u32[]{:S(2)}) collective-permute-start(bf16[16,3072]{1,0:T(8,128)(2,1)S(1)} %add_convert_fusion.4), channel_id=1, source_target_pairs={{0,8},{1,9},{2,10},{3,11},{4,12},{5,13},{6,14},{7,15},{8,0},{9,1},... | collective-permute-start | bytes 294920 | tf_op jit(solution)/shard_map/ppermute | solution.py:33
  125.3 8.0 %collective-permute-start.8 = (bf16[16,64]{1,0:T(8,128)(2,1)S(1)}, bf16[16,64]{1,0:T(8,128)(2,1)S(1)}, u32[]{:S(2)}, u32[]{:S(2)}) collective-permute-start(bf16[16,64]{1,0:T(8,128)(2,1)S(1)} %copy-done.65), channel_id=1, source_target_pairs={{0,8},{1,9},{2,10},{3,11},{4,12},{5,13},{6,14},{7,15},{8,0},{9,1},... | collective-permute-start | bytes 6152 | tf_op jit(solution)/shard_map/ppermute | solution.py:33
  134.3 1.4 collective-permute-start.17
  135.8 7.0 %collective-permute-start.18 = (bf16[32,3072]{1,0:T(8,128)(2,1)S(1)}, bf16[32,3072]{1,0:T(8,128)(2,1)S(1)}, u32[]{:S(2)}, u32[]{:S(2)}) collective-permute-start(bf16[32,3072]{1,0:T(8,128)(2,1)S(1)} %maximum_select_fusion.14), channel_id=1, source_target_pairs={{0,2},{2,0},{1,3},{3,1},{4,6},{6,4},{5,7},{7,5},{8,10},{10,8},{9,1... | collective-permute-start | bytes 589832 | tf_op jit(solution)/shard_map/ppermute | solution.py:28
  142.8 10.5 %collective-permute-start.19 = (bf16[64,3072]{1,0:T(8,128)(2,1)S(1)}, bf16[64,3072]{1,0:T(8,128)(2,1)}, u32[]{:S(2)}, u32[]{:S(2)}) collective-permute-start(bf16[64,3072]{1,0:T(8,128)(2,1)S(1)} %maximum_select_fusion.8), channel_id=1, source_target_pairs={{0,4},{4,0},{1,5},{5,1},{2,6},{6,2},{3,7},{7,3},{8,12},{12,8},{9,1... | collective-permute-start | bytes 1179656 | tf_op jit(solution)/shard_map/ppermute | solution.py:28
  171.8 9.5 %collective-permute-start.20 = (bf16[64,3072]{1,0:T(8,128)(2,1)S(1)}, bf16[64,3072]{1,0:T(8,128)(2,1)S(1)}, u32[]{:S(2)}, u32[]{:S(2)}) collective-permute-start(bf16[64,3072]{1,0:T(8,128)(2,1)S(1)} %select_convert_fusion.3), channel_id=1, source_target_pairs={{0,4},{4,0},{1,5},{5,1},{2,6},{6,2},{3,7},{7,3},{8,12},{12,8},{9,1... | collective-permute-start | bytes 1179656 | tf_op jit(solution)/shard_map/ppermute | solution.py:28
  181.4 5.7 %collective-permute-start.21 = (bf16[32,3072]{1,0:T(8,128)(2,1)S(1)}, bf16[32,3072]{1,0:T(8,128)(2,1)S(1)}, u32[]{:S(2)}, u32[]{:S(2)}) collective-permute-start(bf16[32,3072]{1,0:T(8,128)(2,1)S(1)} %select_convert_fusion.9), channel_id=1, source_target_pairs={{0,2},{2,0},{1,3},{3,1},{4,6},{6,4},{5,7},{7,5},{8,10},{10,8},{9,1... | collective-permute-start | bytes 589832 | tf_op jit(solution)/shard_map/ppermute | solution.py:28
  187.3 1.4 collective-permute-start.22
  188.7 8.1 %collective-permute-start.23 = (bf16[16,3072]{1,0:T(8,128)(2,1)S(1)}, bf16[16,3072]{1,0:T(8,128)(2,1)S(1)}, u32[]{:S(2)}, u32[]{:S(2)}) collective-permute-start(bf16[16,3072]{1,0:T(8,128)(2,1)S(1)} %add_convert_fusion.3), channel_id=1, source_target_pairs={{0,8},{1,9},{2,10},{3,11},{4,12},{5,13},{6,14},{7,15},{8,0},{9,1},... | collective-permute-start | bytes 294920 | tf_op jit(solution)/shard_map/ppermute | solution.py:33
  189.2 8.0 %collective-permute-start.16 = (bf16[16,64]{1,0:T(8,128)(2,1)S(1)}, bf16[16,64]{1,0:T(8,128)(2,1)S(1)}, u32[]{:S(2)}, u32[]{:S(2)}) collective-permute-start(bf16[16,64]{1,0:T(8,128)(2,1)S(1)} %copy-done.66), channel_id=1, source_target_pairs={{0,8},{1,9},{2,10},{3,11},{4,12},{5,13},{6,14},{7,15},{8,0},{9,1},... | collective-permute-start | bytes 6152 | tf_op jit(solution)/shard_map/ppermute | solution.py:33
  198.2 1.4 collective-permute-start.25
  199.6 7.0 %collective-permute-start.26 = (bf16[32,3072]{1,0:T(8,128)(2,1)S(1)}, bf16[32,3072]{1,0:T(8,128)(2,1)S(1)}, u32[]{:S(2)}, u32[]{:S(2)}) collective-permute-start(bf16[32,3072]{1,0:T(8,128)(2,1)S(1)} %maximum_select_fusion.15), channel_id=1, source_target_pairs={{0,2},{2,0},{1,3},{3,1},{4,6},{6,4},{5,7},{7,5},{8,10},{10,8},{9,1... | collective-permute-start | bytes 589832 | tf_op jit(solution)/shard_map/ppermute | solution.py:28
  206.7 10.5 %collective-permute-start.27 = (bf16[64,3072]{1,0:T(8,128)(2,1)S(1)}, bf16[64,3072]{1,0:T(8,128)(2,1)}, u32[]{:S(2)}, u32[]{:S(2)}) collective-permute-start(bf16[64,3072]{1,0:T(8,128)(2,1)S(1)} %maximum_select_fusion.9), channel_id=1, source_target_pairs={{0,4},{4,0},{1,5},{5,1},{2,6},{6,2},{3,7},{7,3},{8,12},{12,8},{9,1... | collective-permute-start | bytes 1179656 | tf_op jit(solution)/shard_map/ppermute | solution.py:28
  235.5 9.5 %collective-permute-start.28 = (bf16[64,3072]{1,0:T(8,128)(2,1)S(1)}, bf16[64,3072]{1,0:T(8,128)(2,1)S(1)}, u32[]{:S(2)}, u32[]{:S(2)}) collective-permute-start(bf16[64,3072]{1,0:T(8,128)(2,1)S(1)} %select_convert_fusion.2), channel_id=1, source_target_pairs={{0,4},{4,0},{1,5},{5,1},{2,6},{6,2},{3,7},{7,3},{8,12},{12,8},{9,1... | collective-permute-start | bytes 1179656 | tf_op jit(solution)/shard_map/ppermute | solution.py:28
  245.2 5.7 %collective-permute-start.29 = (bf16[32,3072]{1,0:T(8,128)(2,1)S(1)}, bf16[32,3072]{1,0:T(8,128)(2,1)S(1)}, u32[]{:S(2)}, u32[]{:S(2)}) collective-permute-start(bf16[32,3072]{1,0:T(8,128)(2,1)S(1)} %select_convert_fusion.8), channel_id=1, source_target_pairs={{0,2},{2,0},{1,3},{3,1},{4,6},{6,4},{5,7},{7,5},{8,10},{10,8},{9,1... | collective-permute-start | bytes 589832 | tf_op jit(solution)/shard_map/ppermute | solution.py:28
  251.0 1.4 collective-permute-start.30
  252.4 8.1 %collective-permute-start.31 = (bf16[16,3072]{1,0:T(8,128)(2,1)S(1)}, bf16[16,3072]{1,0:T(8,128)(2,1)S(1)}, u32[]{:S(2)}, u32[]{:S(2)}) collective-permute-start(bf16[16,3072]{1,0:T(8,128)(2,1)S(1)} %add_convert_fusion.2), channel_id=1, source_target_pairs={{0,8},{1,9},{2,10},{3,11},{4,12},{5,13},{6,14},{7,15},{8,0},{9,1},... | collective-permute-start | bytes 294920 | tf_op jit(solution)/shard_map/ppermute | solution.py:33
  252.9 8.0 %collective-permute-start.24 = (bf16[16,64]{1,0:T(8,128)(2,1)S(1)}, bf16[16,64]{1,0:T(8,128)(2,1)S(1)}, u32[]{:S(2)}, u32[]{:S(2)}) collective-permute-start(bf16[16,64]{1,0:T(8,128)(2,1)S(1)} %copy-done.67), channel_id=1, source_target_pairs={{0,8},{1,9},{2,10},{3,11},{4,12},{5,13},{6,14},{7,15},{8,0},{9,1},... | collective-permute-start | bytes 6152 | tf_op jit(solution)/shard_map/ppermute | solution.py:33
  262.0 1.4 collective-permute-start.33
  263.4 7.0 %collective-permute-start.34 = (bf16[32,3072]{1,0:T(8,128)(2,1)S(1)}, bf16[32,3072]{1,0:T(8,128)(2,1)S(1)}, u32[]{:S(2)}, u32[]{:S(2)}) collective-permute-start(bf16[32,3072]{1,0:T(8,128)(2,1)S(1)} %maximum_select_fusion.16), channel_id=1, source_target_pairs={{0,2},{2,0},{1,3},{3,1},{4,6},{6,4},{5,7},{7,5},{8,10},{10,8},{9,1... | collective-permute-start | bytes 589832 | tf_op jit(solution)/shard_map/ppermute | solution.py:28
  270.5 10.5 %collective-permute-start.35 = (bf16[64,3072]{1,0:T(8,128)(2,1)S(1)}, bf16[64,3072]{1,0:T(8,128)(2,1)}, u32[]{:S(2)}, u32[]{:S(2)}) collective-permute-start(bf16[64,3072]{1,0:T(8,128)(2,1)S(1)} %maximum_select_fusion.10), channel_id=1, source_target_pairs={{0,4},{4,0},{1,5},{5,1},{2,6},{6,2},{3,7},{7,3},{8,12},{12,8},{9,1... | collective-permute-start | bytes 1179656 | tf_op jit(solution)/shard_map/ppermute | solution.py:28
  299.4 9.5 %collective-permute-start.36 = (bf16[64,3072]{1,0:T(8,128)(2,1)S(1)}, bf16[64,3072]{1,0:T(8,128)(2,1)S(1)}, u32[]{:S(2)}, u32[]{:S(2)}) collective-permute-start(bf16[64,3072]{1,0:T(8,128)(2,1)S(1)} %select_convert_fusion.1), channel_id=1, source_target_pairs={{0,4},{4,0},{1,5},{5,1},{2,6},{6,2},{3,7},{7,3},{8,12},{12,8},{9,1... | collective-permute-start | bytes 1179656 | tf_op jit(solution)/shard_map/ppermute | solution.py:28
  309.1 5.7 %collective-permute-start.37 = (bf16[32,3072]{1,0:T(8,128)(2,1)S(1)}, bf16[32,3072]{1,0:T(8,128)(2,1)S(1)}, u32[]{:S(2)}, u32[]{:S(2)}) collective-permute-start(bf16[32,3072]{1,0:T(8,128)(2,1)S(1)} %select_convert_fusion.7), channel_id=1, source_target_pairs={{0,2},{2,0},{1,3},{3,1},{4,6},{6,4},{5,7},{7,5},{8,10},{10,8},{9,1... | collective-permute-start | bytes 589832 | tf_op jit(solution)/shard_map/ppermute | solution.py:28
  315.0 1.4 collective-permute-start.38
  316.4 8.1 %collective-permute-start.39 = (bf16[16,3072]{1,0:T(8,128)(2,1)S(1)}, bf16[16,3072]{1,0:T(8,128)(2,1)S(1)}, u32[]{:S(2)}, u32[]{:S(2)}) collective-permute-start(bf16[16,3072]{1,0:T(8,128)(2,1)S(1)} %add_convert_fusion.1), channel_id=1, source_target_pairs={{0,8},{1,9},{2,10},{3,11},{4,12},{5,13},{6,14},{7,15},{8,0},{9,1},... | collective-permute-start | bytes 294920 | tf_op jit(solution)/shard_map/ppermute | solution.py:33
  316.8 8.0 %collective-permute-start.32 = (bf16[16,64]{1,0:T(8,128)(2,1)S(1)}, bf16[16,64]{1,0:T(8,128)(2,1)S(1)}, u32[]{:S(2)}, u32[]{:S(2)}) collective-permute-start(bf16[16,64]{1,0:T(8,128)(2,1)S(1)} %copy-done.68), channel_id=1, source_target_pairs={{0,8},{1,9},{2,10},{3,11},{4,12},{5,13},{6,14},{7,15},{8,0},{9,1},... | collective-permute-start | bytes 6152 | tf_op jit(solution)/shard_map/ppermute | solution.py:33
  325.9 1.4 collective-permute-start.41
  327.3 7.0 %collective-permute-start.42 = (bf16[32,3072]{1,0:T(8,128)(2,1)S(1)}, bf16[32,3072]{1,0:T(8,128)(2,1)S(1)}, u32[]{:S(2)}, u32[]{:S(2)}) collective-permute-start(bf16[32,3072]{1,0:T(8,128)(2,1)S(1)} %maximum_select_fusion.17), channel_id=1, source_target_pairs={{0,2},{2,0},{1,3},{3,1},{4,6},{6,4},{5,7},{7,5},{8,10},{10,8},{9,1... | collective-permute-start | bytes 589832 | tf_op jit(solution)/shard_map/ppermute | solution.py:28
  334.4 10.5 %collective-permute-start.43 = (bf16[64,3072]{1,0:T(8,128)(2,1)S(1)}, bf16[64,3072]{1,0:T(8,128)(2,1)}, u32[]{:S(2)}, u32[]{:S(2)}) collective-permute-start(bf16[64,3072]{1,0:T(8,128)(2,1)S(1)} %maximum_select_fusion.11), channel_id=1, source_target_pairs={{0,4},{4,0},{1,5},{5,1},{2,6},{6,2},{3,7},{7,3},{8,12},{12,8},{9,1... | collective-permute-start | bytes 1179656 | tf_op jit(solution)/shard_map/ppermute | solution.py:28
  363.1 9.5 %collective-permute-start.44 = (bf16[64,3072]{1,0:T(8,128)(2,1)S(1)}, bf16[64,3072]{1,0:T(8,128)(2,1)S(1)}, u32[]{:S(2)}, u32[]{:S(2)}) collective-permute-start(bf16[64,3072]{1,0:T(8,128)(2,1)S(1)} %select_convert_fusion), channel_id=1, source_target_pairs={{0,4},{4,0},{1,5},{5,1},{2,6},{6,2},{3,7},{7,3},{8,12},{12,8},{9,1... | collective-permute-start | bytes 1179656 | tf_op jit(solution)/shard_map/ppermute | solution.py:28
  372.8 5.7 %collective-permute-start.45 = (bf16[32,3072]{1,0:T(8,128)(2,1)S(1)}, bf16[32,3072]{1,0:T(8,128)(2,1)S(1)}, u32[]{:S(2)}, u32[]{:S(2)}) collective-permute-start(bf16[32,3072]{1,0:T(8,128)(2,1)S(1)} %select_convert_fusion.6), channel_id=1, source_target_pairs={{0,2},{2,0},{1,3},{3,1},{4,6},{6,4},{5,7},{7,5},{8,10},{10,8},{9,1... | collective-permute-start | bytes 589832 | tf_op jit(solution)/shard_map/ppermute | solution.py:28
  378.6 1.4 collective-permute-start.46
  380.1 8.1 %collective-permute-start.47 = (bf16[16,3072]{1,0:T(8,128)(2,1)S(1)}, bf16[16,3072]{1,0:T(8,128)(2,1)S(1)}, u32[]{:S(2)}, u32[]{:S(2)}) collective-permute-start(bf16[16,3072]{1,0:T(8,128)(2,1)S(1)} %add_convert_fusion), channel_id=1, source_target_pairs={{0,8},{1,9},{2,10},{3,11},{4,12},{5,13},{6,14},{7,15},{8,0},{9,1},... | collective-permute-start | bytes 294920 | tf_op jit(solution)/shard_map/ppermute | solution.py:33
  380.5 8.0 %collective-permute-start.40 = (bf16[16,64]{1,0:T(8,128)(2,1)S(1)}, bf16[16,64]{1,0:T(8,128)(2,1)S(1)}, u32[]{:S(2)}, u32[]{:S(2)}) collective-permute-start(bf16[16,64]{1,0:T(8,128)(2,1)S(1)} %copy-done.64), channel_id=1, source_target_pairs={{0,8},{1,9},{2,10},{3,11},{4,12},{5,13},{6,14},{7,15},{8,0},{9,1},... | collective-permute-start | bytes 6152 | tf_op jit(solution)/shard_map/ppermute | solution.py:33
  (70 other events, 845.3 us)
where the time goes:
time: 392 us; the launch traced here: 390 us
  waiting for transfers between devices  198 us (51%)
  matrix products  78.3 us (20%)
  starting transfers between devices  44.6 us (11%)
  other arithmetic  35.8 us (9%)
  local copies, waits for them, and re-layouts  20.7 us (5%)
  between operations  13.2 us (3%)
    ppermute x36, waiting for transfers between devices, partner(): return lax.ppermute(block, axis, route)  166 us
    ppermute x12, waiting for transfers between devices, from_behind(): lax.ppermute(value, axis, [(i, (i + by) % size) for i in range(size)])  31.8 us
    ppermute x36, starting transfers between devices, partner(): return lax.ppermute(block, axis, route)  25.7 us
    dot_general x6, matrix products, head_terms_of(): jnp.dot(normed, w_qkv[0], preferred_element_type=jnp.float32)  21.7 us
    ppermute x12, starting transfers between devices, from_behind(): lax.ppermute(value, axis, [(i, (i + by) % size) for i in range(size)])  18.9 us
    dot_general x6, matrix products, head_terms_of(): jnp.dot(normed, w_qkv[1], preferred_element_type=jnp.float32)  16.8 us
    dot_general x6, matrix products, head_terms_of(): fresh_values = jnp.dot(normed, w_qkv[2], preferred_element_type=jnp.float32)  15.2 us
    dot_general x2, local copies, waits for them, and re-layouts, head_terms_of(): jnp.dot(normed, w_qkv[0], preferred_element_type=jnp.float32)  9.44 us
  transfers between devices with their start and end apart: 48, of which 39 were waited for; matrix products, arithmetic and copies ran while one was open for 6% of the time, Pallas kernels for 0%

commit v1 on v0

v1 whole, which is shorter than its diff:
```python
import functools
import math

import jax
import jax.numpy as jnp
from jax import lax
from jax.experimental import pallas as pl
from jax.experimental.pallas import tpu as pltpu
from jax.sharding import PartitionSpec as P

HS = 128
GROUP = 8
CHIPS = GROUP // 2
CHUNKS = 4
LANES = 128
EPS = 1e-06
F32 = jnp.float32
BF16 = jnp.bfloat16
MESH = pl.DeviceIdType.MESH


def wait_for(ref, sem):
    pltpu.make_async_copy(ref, ref, sem).wait()


def kernel(
    sections,
    hid, lat, wqkv, wout, kv, gain, mod, fmod, wfin, wemb, flow,
    hout, lout,
    X, Z, W, WO, KV, WE, WF, PF, SB, RB, CB, CR, OWN, R, ZS,
    load_sem, sib_sem, cross_sem, ag_sem, agsib_sem, relay_sem, z_sem, send_sem,
):
    ticks = flow.shape[0]
    rows, depth = hid.shape
    latents = lat.shape[1]
    width = wqkv.shape[2]
    total = kv.shape[1]
    tokens = rows * GROUP
    heads = width // HS
    step = depth // CHUNKS
    cols = [pl.ds(c * step, step) for c in range(CHUNKS)]

    me = lax.axis_index("section")
    sec = me // GROUP
    pos = me % GROUP
    core = pos % 2
    chip = pos // 2
    base = sec * GROUP
    sibling = base + chip * 2 + 1 - core
    low, high = chip % 2, chip // 2
    others = [chip + 1 - 2 * low, chip + 2 - 4 * high, 3 - chip]
    cross = [base + o * 2 + core for o in others]
    first = sec == 0
    last = sec == sections - 1
    after = (me + GROUP) % (sections * GROUP)
    before = (me + (sections - 1) * GROUP) % (sections * GROUP)
    last_base = (sections - 1) * GROUP

    def remote(src, dst, send, recv, target):
        return pltpu.make_async_remote_copy(
            src_ref=src, dst_ref=dst, send_sem=send, recv_sem=recv,
            device_id={"section": target}, device_id_type=MESH,
        )

    loads = [
        pltpu.make_async_copy(hid, X.at[0, pos], load_sem.at[0]),
        pltpu.make_async_copy(wqkv.at[0], W.at[:, pl.ds(0, width)], load_sem.at[1]),
        pltpu.make_async_copy(wqkv.at[1], W.at[:, pl.ds(width, width)], load_sem.at[2]),
        pltpu.make_async_copy(wqkv.at[2], W.at[:, pl.ds(2 * width, width)], load_sem.at[3]),
        pltpu.make_async_copy(kv, KV, load_sem.at[4]),
        pltpu.make_async_copy(wout, WO, load_sem.at[5]),
        pltpu.make_async_copy(wemb, WE, load_sem.at[6]),
        pltpu.make_async_copy(wfin, WF, load_sem.at[7]),
    ]
    for load in loads:
        load.start()

    barrier = pltpu.get_barrier_semaphore()

    def greet(target):
        pl.semaphore_signal(barrier, inc=1, device_id={"section": target}, device_id_type=MESH)

    greet(sibling)
    for target in cross:
        greet(target)

    @pl.when(first)
    def _():
        for i in range(GROUP):
            greet(last_base + i)

    @pl.when(last)
    def _():
        for i in range(GROUP):
            greet(i)

    if sections > 2:

        @pl.when(jnp.logical_not(last))
        def _():
            greet(after)

        @pl.when(jnp.logical_not(first))
        def _():
            greet(before)

    if sections == 2:
        pl.semaphore_wait(barrier, CHIPS + GROUP)
    else:
        edge = jnp.logical_or(first, last)

        @pl.when(edge)
        def _():
            pl.semaphore_wait(barrier, CHIPS + GROUP + 1)

        @pl.when(jnp.logical_not(edge))
        def _():
            pl.semaphore_wait(barrier, CHIPS + 2)

    ZS[...] = jnp.zeros_like(ZS)
    Z[0, pos] = jnp.zeros((rows, LANES), BF16)
    Z[0, pos, :, 0:latents] = lat[...]
    loads[0].wait()

    def embed(z, c):
        return jnp.dot(z, WE[:, cols[c]], preferred_element_type=F32).astype(BF16)

    def gather(t):
        def forward(c):
            wait_for(X.at[t, pl.ds(0, 3), :, cols[c]], ag_sem.at[c])
            for o in others:
                block = X.at[t, o * 2 + core, :, cols[c]]
                remote(block, block, send_sem.at[0], agsib_sem, sibling).start()

        for c in range(CHUNKS):

            @pl.when(t > 0)
            def _():
                wait_for(X.at[t, pos, :, cols[c]], relay_sem.at[t, c])

            block = X.at[t, pos, :, cols[c]]
            for target in cross:
                remote(block, block, send_sem.at[0], ag_sem.at[c], target).start()
            remote(block, block, send_sem.at[0], agsib_sem, sibling).start()
            if c > 0:
                forward(c - 1)
        forward(CHUNKS - 1)
        wait_for(X.at[t, pl.ds(0, CHIPS)], agsib_sem)
        wait_for(X.at[t, pl.ds(0, GROUP - 1)], send_sem.at[0])

    def tick(t, carry):
        par = t % 2

        @pl.when(jnp.logical_and(t > 0, first))
        def _():
            wait_for(Z.at[t], z_sem.at[t])
            z = Z[t].reshape(tokens, LANES)[:, :latents]
            for c in range(CHUNKS):
                X[t, :, :, cols[c]] = embed(z, c).reshape(GROUP, rows, step)

        @pl.when(jnp.logical_and(t > 0, jnp.logical_not(first)))
        def _():
            wait_for(Z.at[t, pos], z_sem.at[t])

        @pl.when(jnp.logical_or(t == 0, jnp.logical_not(first)))
        def _():
            gather(t)

        @pl.when(t == 0)
        def _():
            for load in loads[1:]:
                load.wait()

        def part(c):
            return X[t, :, :, cols[c]].reshape(tokens, step).astype(F32)

        mean = sum(jnp.sum(part(c), axis=-1, keepdims=True) for c in range(CHUNKS)) / depth
        variance = (
            sum(
                jnp.sum(jnp.square(part(c) - mean), axis=-1, keepdims=True) for c in range(CHUNKS)
            )
            / depth
        )
        inverse = lax.rsqrt(variance + EPS)
        qkv = None
        for c in range(CHUNKS):
            normed = (
                (part(c) - mean) * inverse * (1.0 + mod[sec, 1:2, cols[c]])
                + mod[sec, 0:1, cols[c]]
            ).astype(BF16)
            term = jnp.dot(normed, W[cols[c], :], preferred_element_type=F32)
            qkv = term if qkv is None else qkv + term

        def head_norm(v, g):
            return (
                v * lax.rsqrt(jnp.mean(v * v, axis=-1, keepdims=True) + EPS) * g
            ).astype(BF16)

        patch = flow[t, sec]
        outs = []
        for h in range(heads):
            at = slice(h * HS, (h + 1) * HS)
            qn = head_norm(qkv[:, at], gain[sec, 0:1, :])
            kn = head_norm(qkv[:, width + h * HS : width + (h + 1) * HS], gain[sec, 1:2, :])
            vb = qkv[:, 2 * width + h * HS : 2 * width + (h + 1) * HS].astype(BF16)
            for which, fresh in ((0, kn), (1, vb)):
                for j in range(total // tokens):
                    place = slice(j * tokens, (j + 1) * tokens)
                    KV[which, place, at] = jnp.where(
                        patch == j, fresh.astype(F32), KV[which, place, at].astype(F32)
                    ).astype(BF16)
            scores = lax.dot_general(
                qn, KV[0, :, at], (((1,), (1,)), ((), ())), preferred_element_type=F32
            ) * (1.0 / math.sqrt(HS))
            e = jnp.exp(scores)
            totals = jnp.sum(e, axis=-1, keepdims=True)
            mixed = jnp.dot(e.astype(BF16), KV[1, :, at], preferred_element_type=F32)
            outs.append((mixed / totals).astype(BF16))
        attended = jnp.concatenate(outs, axis=1)

        for c in range(CHUNKS):
            product = jnp.dot(attended, WO[:, cols[c]], preferred_element_type=F32)
            product = product.reshape(CHIPS, 2, rows, step)
            for side in range(2):
                PF[side, :, :, cols[c]] = product[:, side]
            SB[:, :, cols[c]] = PF[1 - core, :, :, cols[c]].astype(BF16)
            remote(
                SB.at[:, :, cols[c]], RB.at[par, :, :, cols[c]],
                send_sem.at[1], sib_sem.at[par, c], sibling,
            ).start()

        for c in range(CHUNKS):
            wait_for(RB.at[par, :, :, cols[c]], sib_sem.at[par, c])
            both = PF[core, :, :, cols[c]] + RB[par, :, :, cols[c]].astype(F32)
            PF[core, :, :, cols[c]] = both
            CB[:, :, cols[c]] = both.astype(BF16)
            for r in range(CHIPS - 1):
                remote(
                    CB.at[others[r], :, cols[c]], CR.at[par, r, :, cols[c]],
                    send_sem.at[2], cross_sem.at[par, c], cross[r],
                ).start()

        for c in range(CHUNKS):
            wait_for(CR.at[par, :, :, cols[c]], cross_sem.at[par, c])
            summed = PF[core, chip, :, cols[c]]
            for r in range(CHIPS - 1):
                summed = summed + CR[par, r, :, cols[c]].astype(F32)
            result = X[t, pos, :, cols[c]].astype(F32) + mod[sec, 2:3, cols[c]] * summed
            R[:, cols[c]] = result.astype(BF16)

            @pl.when(jnp.logical_not(last))
            def _():
                remote(
                    R.at[:, cols[c]], X.at[t + 1, pos, :, cols[c]],
                    send_sem.at[3], relay_sem.at[t + 1, c], after,
                ).start()

        @pl.when(jnp.logical_not(last))
        def _():
            copy = remote(Z.at[t, pos], Z.at[t + 1, pos], send_sem.at[4], z_sem.at[t + 1], after)
            copy.start()
            wait_for(Z.at[t, pos], send_sem.at[4])
            wait_for(R, send_sem.at[3])

        @pl.when(last)
        def _():
            x = R[...].astype(F32)
            centred = x - jnp.mean(x, axis=-1, keepdims=True)
            spread = jnp.mean(centred * centred, axis=-1, keepdims=True)
            normed = (
                centred * lax.rsqrt(spread + EPS) * (1.0 + fmod[1:2, :]) + fmod[0:1, :]
            ).astype(BF16)
            velocity = jnp.dot(normed, WF[...], preferred_element_type=F32)
            ZS[:, 0:latents] = (Z[t, pos][:, :latents].astype(F32) + velocity).astype(BF16)
            for i in range(GROUP):
                remote(ZS, Z.at[t + 1, pos], send_sem.at[4], z_sem.at[t + 1], i).start()
            wait_for(Z.at[t], send_sem.at[4])

        wait_for(SB, send_sem.at[1])
        wait_for(CR.at[par], send_sem.at[2])
        return carry

    lax.fori_loop(0, ticks, tick, 0)

    @pl.when(first)
    def _():
        wait_for(Z.at[ticks], z_sem.at[ticks])
        z = Z[ticks, pos][:, :latents]
        for c in range(CHUNKS):
            hout[:, cols[c]] = embed(z, c)

    @pl.when(jnp.logical_not(first))
    def _():
        wait_for(Z.at[ticks, pos], z_sem.at[ticks])
        for c in range(CHUNKS):
            wait_for(X.at[ticks, pos, :, cols[c]], relay_sem.at[ticks, c])
        hout[...] = X[ticks, pos]

    lout[...] = Z[ticks, pos][:, :latents]


def body(
    sections, hidden_in, latent_in, w_qkv, w_out, stale_kv, qk_gain, block_mod, final_mod,
    w_final, w_embed, patch_flow,
):
    rows, depth = hidden_in.shape
    latents = latent_in.shape[1]
    width = w_qkv.shape[2]
    ticks = patch_flow.shape[0]
    anywhere = pl.BlockSpec(memory_space=pl.ANY)
    vmem = pl.BlockSpec(memory_space=pltpu.VMEM)
    smem = pl.BlockSpec(memory_space=pltpu.SMEM)
    dma = pltpu.SemaphoreType.DMA
    macs = ticks * rows * GROUP * depth * width * 4
    return pl.pallas_call(
        functools.partial(kernel, sections),
        out_shape=(
            jax.ShapeDtypeStruct((rows, depth), BF16),
            jax.ShapeDtypeStruct((rows, latents), BF16),
        ),
        in_specs=[
            anywhere, vmem, anywhere, anywhere, anywhere, vmem, vmem, vmem, anywhere, anywhere,
            smem,
        ],
        out_specs=(vmem, vmem),
        scratch_shapes=[
            pltpu.VMEM((ticks + 1, GROUP, rows, depth), BF16),
            pltpu.VMEM((ticks + 1, GROUP, rows, LANES), BF16),
            pltpu.VMEM((depth, 3 * width), BF16),
            pltpu.VMEM((width, depth), BF16),
            pltpu.VMEM(stale_kv.shape, BF16),
            pltpu.VMEM(w_embed.shape, BF16),
            pltpu.VMEM(w_final.shape, BF16),
            pltpu.VMEM((2, CHIPS, rows, depth), F32),
            pltpu.VMEM((CHIPS, rows, depth), BF16),
            pltpu.VMEM((2, CHIPS, rows, depth), BF16),
            pltpu.VMEM((CHIPS, rows, depth), BF16),
            pltpu.VMEM((2, CHIPS - 1, rows, depth), BF16),
            pltpu.VMEM((rows, depth), F32),
            pltpu.VMEM((rows, depth), BF16),
            pltpu.VMEM((rows, LANES), BF16),
            dma((8,)),
            dma((2, CHUNKS)),
            dma((2, CHUNKS)),
            dma((CHUNKS,)),
            dma,
            dma((ticks + 1, CHUNKS)),
            dma((ticks + 1,)),
            dma((5,)),
        ],
        compiler_params=pltpu.CompilerParams(
            collective_id=0, has_side_effects=True, vmem_limit_bytes=52 * 1024 * 1024
        ),
        cost_estimate=pl.CostEstimate(flops=2 * macs, bytes_accessed=10**7, transcendentals=0),
    )(
        hidden_in, latent_in, w_qkv, w_out, stale_kv, qk_gain, block_mod, final_mod,
        w_final, w_embed, patch_flow,
    )


def solution(mesh):
    in_specs = (
        P(("groups", "section"), None),
        P(("groups", "section"), None),
        P(None, None, "section"),
        P("section", None),
        P("groups", None, "section"),
        P(),
        P("groups", None, None),
        P("groups", None),
        P(),
        P(),
        P(),
    )
    out_specs = (P(("groups", "section"), None), P(("groups", "section"), None))
    sections = mesh.shape["section"] // GROUP
    return jax.shard_map(
        functools.partial(body, sections), mesh=mesh, in_specs=in_specs, out_specs=out_specs,
        check_vma=False,
    )
```

time: 392 us -> 154 us (0.39)
  waiting for transfers between devices: 198 us -> 0 us
  Pallas kernels: 0 us -> 143 us
  matrix products: 78.3 us -> 0 us
  starting transfers between devices: 44.6 us -> 0 us
  other arithmetic: 35.8 us -> 0 us
  between operations: 13.2 us -> 0.66 us
  local copies, waits for them, and re-layouts: 20.7 us -> 9.28 us
    ppermute x48 -> x0, waiting for transfers between devices: 198 us -> none  [the longest x36 166 us: partner(): return lax.ppermute(block, axis, route)]
    pallas_call x0 -> x1, Pallas kernels: none -> 143 us  [body(): pl.pallas_call(functools.partial(kernel, sections), out_shape=(jax.ShapeD...]
    dot_general x48 -> x0, matrix products: 78.3 us -> none  [the longest x6 21.7 us: head_terms_of(): jnp.dot(normed, w_qkv[0], preferred_element_type=jnp.float32)]
    ppermute x48 -> x0, starting transfers between devices: 44.6 us -> none  [the longest x36 25.7 us: partner(): return lax.ppermute(block, axis, route)]
    reduce_sum x24 -> x0, other arithmetic: 17.2 us -> none  [the longest x12 9.21 us: layer_norm(): variance = jnp.mean(centred * centred, axis=-1, keepdims=True)]
    dot_general x3 -> x0, local copies, waits for them, and re-layouts: 13.7 us -> none  [the longest x2 9.44 us: head_terms_of(): jnp.dot(normed, w_qkv[0], preferred_element_type=jnp.float32)]
    unnamed x142 -> x17, local copies, waits for them, and re-layouts: 1.29 us -> 9.28 us
    rsqrt x24 -> x0, other arithmetic: 6.66 us -> none  [the longest x12 6.56 us: head_norm(): lax.rsqrt(jnp.mean(values * values, axis=-1, keepdims=True) + 1e-06)]
  transfers between devices with their start and end apart: 48 -> 0, of which waited for: 39 -> 0; matrix products, arithmetic and copies ran while one was open for 6% -> 0% of each run, Pallas kernels for 0% -> 0%
where the time goes in v1:
time: 154 us; the launch traced here: 153 us
  Pallas kernels  143 us (93%)
  local copies, waits for them, and re-layouts  9.28 us (6%)
    pallas_call x1, Pallas kernels, body(): pl.pallas_call(functools.partial(kernel, sections), out_shape=(jax.ShapeD...  143 us
    unnamed x17, local copies, waits for them, and re-layouts  9.28 us

profile of v1, /device:TPU:0, one launch (start us, length us, event | category | flops | bytes accessed | tf_op | source)
XLA Modules:
  0.0 153.1 jit_solution(8629188694825943043)
XLA Ops:
  0.6 0.8 copy.15.flow
  1.4 0.9 copy.13.mod
  2.3 1.4 copy.14.wfin
  3.7 0.0 copy-start
  3.7 1.0 copy-done
  4.7 0.0 copy-start.1
  4.7 1.0 copy-done.1
  5.7 0.0 copy-start.2
  5.7 0.9 copy-done.2
  6.6 0.0 copy-start.3
  6.6 0.7 copy-done.3
  7.3 0.0 copy-start.4
  7.3 0.7 copy-done.4
  8.0 0.0 copy-start.5
  8.0 0.7 copy-done.5
  8.7 143.1 %shard_map.122 = (bf16[16,3072]{1,0:T(8,128)(2,1)S(1)}, bf16[16,64]{1,0:T(8,128)(2,1)S(1)}) custom-call(bf16[16,3072]{1,0:T(8,128)(2,1)S(1)} %copy-done.2, bf16[16,64]{1,0:T(8,128)(2,1)S(1)} %copy-done.4, bf16[3,3072,384]{2,1,0:T(8,128)(2,1)} %wqkv.1, bf16[384,3072]{1,0:T(8,128)(2,1)} %wout.1, bf16[2,256,384]{2,1,0:T(8,128)(2,1)S(1)} %copy-done, ...), custom_call_target="tpu_custom_call" | custom-call | flops 7247757312 | bytes 10000000 | tf_op jit(solution)/shard_map/pallas_call | solution.py:315
  151.8 0.6 copy.18
  152.5 0.6 copy.19
Async XLA Ops:
  3.7 1.0 copy-start
  4.7 1.0 copy-start.1
  5.7 0.9 copy-start.2
  6.6 0.7 copy-start.3
  7.3 0.7 copy-start.4
  8.0 0.7 copy-start.5

commit v2 on v1

--- a/solution.py
+++ b/solution.py
@@ -12,7 +12,7 @@
 GROUP = 8
 CHIPS = GROUP // 2
 CHUNKS = 4
-LANES = 128
+EXTRA = 16
 EPS = 1e-06
 F32 = jnp.float32
 BF16 = jnp.bfloat16
@@ -25,14 +25,16 @@
 
 def kernel(
     sections,
-    hid, lat, wqkv, wout, kv, gain, mod, fmod, wfin, wemb, flow,
+    hid, lat, wqkv, wout, kv, gain_in, mod_in, fmod_in, wfin, wemb, flow,
     hout, lout,
-    X, Z, W, WO, KV, WE, WF, PF, SB, RB, CB, CR, OWN, R, ZS,
+    X, Z, W, WO, KV, WE, WF, PF, SB, RB, CB, CR, R, ZS,
+    gain, mod, fmod, LAT, EX, SW, MH, WC, QKV,
     load_sem, sib_sem, cross_sem, ag_sem, agsib_sem, relay_sem, z_sem, send_sem,
 ):
-    ticks = flow.shape[0]
+    ticks = flow.shape[1]
     rows, depth = hid.shape
     latents = lat.shape[1]
+    lanes = 2 * latents
     width = wqkv.shape[2]
     total = kv.shape[1]
     tokens = rows * GROUP
@@ -71,6 +73,10 @@
         pltpu.make_async_copy(wout, WO, load_sem.at[5]),
         pltpu.make_async_copy(wemb, WE, load_sem.at[6]),
         pltpu.make_async_copy(wfin, WF, load_sem.at[7]),
+        pltpu.make_async_copy(gain_in, gain, load_sem.at[8]),
+        pltpu.make_async_copy(fmod_in, fmod, load_sem.at[9]),
+        pltpu.make_async_copy(mod_in, mod, load_sem.at[10]),
+        pltpu.make_async_copy(lat, LAT, load_sem.at[11]),
     ]
     for load in loads:
         load.start()
@@ -117,9 +123,27 @@
         def _():
             pl.semaphore_wait(barrier, CHIPS + 2)
 
-    ZS[...] = jnp.zeros_like(ZS)
-    Z[0, pos] = jnp.zeros((rows, LANES), BF16)
-    Z[0, pos, :, 0:latents] = lat[...]
+    def split(v):
+        high_part = v.astype(BF16)
+        return high_part, (v - high_part.astype(F32)).astype(BF16)
+
+    def param(k, c):
+        return mod[k, pl.ds(sec, 1), cols[c]]
+
+    def prepare():
+        ZS[...] = jnp.zeros_like(ZS)
+        Z[0, pos] = jnp.zeros((rows, lanes), BF16)
+        loads[11].wait()
+        Z[0, pos, :, 0:latents] = LAT[...]
+        loads[10].wait()
+        row = lax.broadcasted_iota(jnp.int32, (EXTRA, step), 0)
+        for c in range(CHUNKS):
+            parts = split(1.0 + param(1, c)) + split(param(0, c))
+            block = jnp.zeros((EXTRA, step), F32)
+            for k, v in enumerate(parts):
+                block = jnp.where(row == k, v.astype(F32), block)
+            EX[:, cols[c]] = block.astype(BF16)
+
     loads[0].wait()
 
     def embed(z, c):
@@ -130,7 +154,23 @@
             wait_for(X.at[t, pl.ds(0, 3), :, cols[c]], ag_sem.at[c])
             for o in others:
                 block = X.at[t, o * 2 + core, :, cols[c]]
-                remote(block, block, send_sem.at[0], agsib_sem, sibling).start()
+                remote(block, block, send_sem.at[0], agsib_sem.at[c], sibling).start()
+
+        def multiply(c, state):
+            wait_for(X.at[t, pl.ds(0, CHIPS), :, cols[c]], agsib_sem.at[c])
+            x = X[t, :, :, cols[c]].reshape(tokens, step).astype(F32)
+            if state is None:
+                start = jnp.mean(x, axis=-1, keepdims=True)
+            else:
+                start = state[0]
+            d = x - start
+            s1 = jnp.sum(d, axis=-1, keepdims=True)
+            s2 = jnp.sum(d * d, axis=-1, keepdims=True)
+            y = jnp.concatenate([(d * (1.0 + param(1, c))).astype(BF16), EX[:, cols[c]]], axis=0)
+            raw = jnp.dot(y, W[cols[c], :], preferred_element_type=F32)
+            if state is None:
+                return start, s1, s2, raw
+            return start, state[1] + s1, state[2] + s2, state[3] + raw
 
         for c in range(CHUNKS):
 
@@ -139,14 +179,58 @@
                 wait_for(X.at[t, pos, :, cols[c]], relay_sem.at[t, c])
 
             block = X.at[t, pos, :, cols[c]]
-            for target in cross:
+            for target in reversed(cross):
                 remote(block, block, send_sem.at[0], ag_sem.at[c], target).start()
-            remote(block, block, send_sem.at[0], agsib_sem, sibling).start()
+            remote(block, block, send_sem.at[0], agsib_sem.at[c], sibling).start()
+            if c == 0:
+
+                @pl.when(t == 0)
+                def _():
+                    prepare()
+
             if c > 0:
                 forward(c - 1)
+            if c == 1:
+
+                @pl.when(t == 0)
+                def _():
+                    for load in loads[1:10]:
+                        load.wait()
+
+            if c > 1:
+                state = multiply(c - 2, state if c > 2 else None)
+        state = multiply(CHUNKS - 2, state)
         forward(CHUNKS - 1)
-        wait_for(X.at[t, pl.ds(0, CHIPS)], agsib_sem)
+        start, s1, s2, raw = multiply(CHUNKS - 1, state)
+        rest = s1 / depth
+        inverse = lax.rsqrt(jnp.maximum(s2 / depth - rest * rest, 0.0) + EPS)
+        scale_sums = raw[tokens : tokens + 1] + raw[tokens + 1 : tokens + 2]
+        shift_sums = raw[tokens + 2 : tokens + 3] + raw[tokens + 3 : tokens + 4]
+        SW[0:1, :] = shift_sums
+        QKV[...] = inverse * (raw[:tokens] - rest * scale_sums) + shift_sums
         wait_for(X.at[t, pl.ds(0, GROUP - 1)], send_sem.at[0])
+
+    def fold():
+        centre = jnp.mean(WE[...].astype(F32), axis=-1, keepdims=True)
+        folded = None
+        for c in range(CHUNKS):
+            w = WE[:, cols[c]].astype(F32) - centre
+            WC[0:latents, cols[c]], WC[latents : 2 * latents, cols[c]] = split(w)
+            term = jnp.dot(
+                (w * (1.0 + param(1, c))).astype(BF16), W[cols[c], :], preferred_element_type=F32
+            )
+            folded = term if folded is None else folded + term
+        MH[0:latents, :], MH[latents : 2 * latents, :] = split(folded)
+
+    def embedded(t):
+        z = Z[t].reshape(tokens, lanes)[:, : 2 * latents]
+        squares = None
+        for c in range(CHUNKS):
+            h = jnp.dot(z, WC[:, cols[c]], preferred_element_type=F32)
+            term = jnp.sum(h * h, axis=-1, keepdims=True)
+            squares = term if squares is None else squares + term
+        inverse = lax.rsqrt(squares / depth + EPS)
+        QKV[...] = inverse * jnp.dot(z, MH[...], preferred_element_type=F32) + SW[0:1, :]
 
     def tick(t, carry):
         par = t % 2
@@ -154,9 +238,7 @@
         @pl.when(jnp.logical_and(t > 0, first))
         def _():
             wait_for(Z.at[t], z_sem.at[t])
-            z = Z[t].reshape(tokens, LANES)[:, :latents]
-            for c in range(CHUNKS):
-                X[t, :, :, cols[c]] = embed(z, c).reshape(GROUP, rows, step)
+            embedded(t)
 
         @pl.when(jnp.logical_and(t > 0, jnp.logical_not(first)))
         def _():
@@ -166,37 +248,14 @@
         def _():
             gather(t)
 
-        @pl.when(t == 0)
-        def _():
-            for load in loads[1:]:
-                load.wait()
-
-        def part(c):
-            return X[t, :, :, cols[c]].reshape(tokens, step).astype(F32)
-
-        mean = sum(jnp.sum(part(c), axis=-1, keepdims=True) for c in range(CHUNKS)) / depth
-        variance = (
-            sum(
-                jnp.sum(jnp.square(part(c) - mean), axis=-1, keepdims=True) for c in range(CHUNKS)
-            )
-            / depth
-        )
-        inverse = lax.rsqrt(variance + EPS)
-        qkv = None
-        for c in range(CHUNKS):
-            normed = (
-                (part(c) - mean) * inverse * (1.0 + mod[sec, 1:2, cols[c]])
-                + mod[sec, 0:1, cols[c]]
-            ).astype(BF16)
-            term = jnp.dot(normed, W[cols[c], :], preferred_element_type=F32)
-            qkv = term if qkv is None else qkv + term
+        qkv = QKV[...]
 
         def head_norm(v, g):
             return (
                 v * lax.rsqrt(jnp.mean(v * v, axis=-1, keepdims=True) + EPS) * g
             ).astype(BF16)
 
-        patch = flow[t, sec]
+        patch = flow[sec, t]
         outs = []
         for h in range(heads):
             at = slice(h * HS, (h + 1) * HS)
@@ -218,7 +277,7 @@
             outs.append((mixed / totals).astype(BF16))
         attended = jnp.concatenate(outs, axis=1)
 
-        for c in range(CHUNKS):
+        def project(c):
             product = jnp.dot(attended, WO[:, cols[c]], preferred_element_type=F32)
             product = product.reshape(CHIPS, 2, rows, step)
             for side in range(2):
@@ -229,23 +288,35 @@
                 send_sem.at[1], sib_sem.at[par, c], sibling,
             ).start()
 
-        for c in range(CHUNKS):
+        def share(c):
             wait_for(RB.at[par, :, :, cols[c]], sib_sem.at[par, c])
             both = PF[core, :, :, cols[c]] + RB[par, :, :, cols[c]].astype(F32)
             PF[core, :, :, cols[c]] = both
             CB[:, :, cols[c]] = both.astype(BF16)
-            for r in range(CHIPS - 1):
+            for r in reversed(range(CHIPS - 1)):
                 remote(
                     CB.at[others[r], :, cols[c]], CR.at[par, r, :, cols[c]],
                     send_sem.at[2], cross_sem.at[par, c], cross[r],
                 ).start()
 
         for c in range(CHUNKS):
+            project(c)
+            if c > 0:
+                share(c - 1)
+        share(CHUNKS - 1)
+
+        @pl.when(jnp.logical_and(t > 0, first))
+        def _():
+            z = Z[t, pos][:, :latents]
+            for c in range(CHUNKS):
+                X[t, pos, :, cols[c]] = embed(z, c)
+
+        for c in range(CHUNKS):
             wait_for(CR.at[par, :, :, cols[c]], cross_sem.at[par, c])
             summed = PF[core, chip, :, cols[c]]
             for r in range(CHIPS - 1):
                 summed = summed + CR[par, r, :, cols[c]].astype(F32)
-            result = X[t, pos, :, cols[c]].astype(F32) + mod[sec, 2:3, cols[c]] * summed
+            result = X[t, pos, :, cols[c]].astype(F32) + param(2, c) * summed
             R[:, cols[c]] = result.astype(BF16)
 
             @pl.when(jnp.logical_not(last))
@@ -270,11 +341,18 @@
             normed = (
                 centred * lax.rsqrt(spread + EPS) * (1.0 + fmod[1:2, :]) + fmod[0:1, :]
             ).astype(BF16)
-            velocity = jnp.dot(normed, WF[...], preferred_element_type=F32)
-            ZS[:, 0:latents] = (Z[t, pos][:, :latents].astype(F32) + velocity).astype(BF16)
+            velocity = lax.dot_general(
+                normed, WF[...], (((1,), (1,)), ((), ())), preferred_element_type=F32
+            )
+            renewed = (Z[t, pos][:, :latents].astype(F32) + velocity).astype(BF16)
+            ZS[...] = jnp.concatenate([renewed, renewed], axis=1)
             for i in range(GROUP):
                 remote(ZS, Z.at[t + 1, pos], send_sem.at[4], z_sem.at[t + 1], i).start()
             wait_for(Z.at[t], send_sem.at[4])
+
+        @pl.when(jnp.logical_and(t == 0, first))
+        def _():
+            fold()
 
         wait_for(SB, send_sem.at[1])
         wait_for(CR.at[par], send_sem.at[2])
@@ -305,9 +383,10 @@
 ):
     rows, depth = hidden_in.shape
     latents = latent_in.shape[1]
+    lanes = 2 * latents
     width = w_qkv.shape[2]
     ticks = patch_flow.shape[0]
-    anywhere = pl.BlockSpec(memory_space=pl.ANY)
+    anywhere = pl.BlockSpec(memory_space=pltpu.HBM)
     vmem = pl.BlockSpec(memory_space=pltpu.VMEM)
     smem = pl.BlockSpec(memory_space=pltpu.SMEM)
     dma = pltpu.SemaphoreType.DMA
@@ -319,42 +398,50 @@
             jax.ShapeDtypeStruct((rows, latents), BF16),
         ),
         in_specs=[
-            anywhere, vmem, anywhere, anywhere, anywhere, vmem, vmem, vmem, anywhere, anywhere,
-            smem,
+            anywhere, anywhere, anywhere, anywhere, anywhere, anywhere, anywhere, anywhere,
+            anywhere, anywhere, smem,
         ],
         out_specs=(vmem, vmem),
         scratch_shapes=[
             pltpu.VMEM((ticks + 1, GROUP, rows, depth), BF16),
-            pltpu.VMEM((ticks + 1, GROUP, rows, LANES), BF16),
+            pltpu.VMEM((ticks + 1, GROUP, rows, lanes), BF16),
             pltpu.VMEM((depth, 3 * width), BF16),
             pltpu.VMEM((width, depth), BF16),
             pltpu.VMEM(stale_kv.shape, BF16),
             pltpu.VMEM(w_embed.shape, BF16),
-            pltpu.VMEM(w_final.shape, BF16),
+            pltpu.VMEM((latents, depth), BF16),
             pltpu.VMEM((2, CHIPS, rows, depth), F32),
             pltpu.VMEM((CHIPS, rows, depth), BF16),
             pltpu.VMEM((2, CHIPS, rows, depth), BF16),
             pltpu.VMEM((CHIPS, rows, depth), BF16),
             pltpu.VMEM((2, CHIPS - 1, rows, depth), BF16),
-            pltpu.VMEM((rows, depth), F32),
             pltpu.VMEM((rows, depth), BF16),
-            pltpu.VMEM((rows, LANES), BF16),
-            dma((8,)),
+            pltpu.VMEM((rows, lanes), BF16),
+            pltpu.VMEM(qk_gain.shape, F32),
+            pltpu.VMEM((3, sections, depth), F32),
+            pltpu.VMEM(final_mod.shape, F32),
+            pltpu.VMEM((rows, latents), BF16),
+            pltpu.VMEM((EXTRA, depth), BF16),
+            pltpu.VMEM((8, 3 * width), F32),
+            pltpu.VMEM((lanes, 3 * width), BF16),
+            pltpu.VMEM((lanes, depth), BF16),
+            pltpu.VMEM((rows * GROUP, 3 * width), F32),
+            dma((12,)),
             dma((2, CHUNKS)),
             dma((2, CHUNKS)),
             dma((CHUNKS,)),
-            dma,
+            dma((CHUNKS,)),
             dma((ticks + 1, CHUNKS)),
             dma((ticks + 1,)),
             dma((5,)),
         ],
         compiler_params=pltpu.CompilerParams(
-            collective_id=0, has_side_effects=True, vmem_limit_bytes=52 * 1024 * 1024
+            collective_id=0, has_side_effects=True, vmem_limit_bytes=64 * 1024 * 1024
         ),
         cost_estimate=pl.CostEstimate(flops=2 * macs, bytes_accessed=10**7, transcendentals=0),
     )(
-        hidden_in, latent_in, w_qkv, w_out, stale_kv, qk_gain, block_mod, final_mod,
-        w_final, w_embed, patch_flow,
+        hidden_in, latent_in, w_qkv, w_out, stale_kv, qk_gain,
+        jnp.transpose(block_mod, (1, 0, 2)), final_mod, w_final.T, w_embed, patch_flow.T,
     )
 
 

time: 154 us -> 142 us (0.922)
  local copies, waits for them, and re-layouts: 9.28 us -> 2.81 us
  Pallas kernels: 143 us -> 138 us
    unnamed x17 -> x2, local copies, waits for them, and re-layouts: 9.28 us -> 2.81 us
    pallas_call x1, Pallas kernels: 143 us -> 138 us  [body(): pl.pallas_call(functools.partial(kernel, sections), out_shape=(jax.ShapeD...]
where the time goes in v2:
time: 142 us
  Pallas kernels  138 us (97%)
  local copies, waits for them, and re-layouts  2.81 us (2%)
    pallas_call x1, Pallas kernels, body(): pl.pallas_call(functools.partial(kernel, sections), out_shape=(jax.ShapeD...  138 us

profile of v2, /device:TPU:0, one launch (start us, length us, event | category | flops | bytes accessed | tf_op | source)
XLA Modules:
  0.0 141.6 jit_solution(5102638556934870339)
XLA Ops:
  0.6 138.2 %shard_map.122 = (bf16[16,3072]{1,0:T(8,128)(2,1)}, bf16[16,64]{1,0:T(8,128)(2,1)}) custom-call(bf16[16,3072]{1,0:T(8,128)(2,1)} %hid.1, bf16[16,64]{1,0:T(8,128)(2,1)} %lat.1, bf16[3,3072,384]{2,1,0:T(8,128)(2,1)} %wqkv.1, bf16[384,3072]{1,0:T(8,128)(2,1)} %wout.1, bf16[2,256,384]{2,1,0:T(8,128)(2,1)} %kv.1, f32[2,2,128]{2,1,0:T(2,128)} %gain_in.1, ...), custom_call_target="tpu_custom_call" | custom-call | flops 7247757312 | bytes 10000000 | tf_op jit(solution)/shard_map/pallas_call | solution.py:394
  138.8 1.5 %copy.15 = bf16[16,3072]{1,0:T(8,128)(2,1)} copy(bf16[16,3072]{1,0:T(8,128)(2,1)} %get-tuple-element.4) | data formatting | bytes 196608
  140.4 1.3 copy.16

commit v3 on v2

--- a/solution.py
+++ b/solution.py
@@ -11,8 +11,9 @@
 HS = 128
 GROUP = 8
 CHIPS = GROUP // 2
-CHUNKS = 4
+CHUNKS = 3
 EXTRA = 16
+LAG = 2
 EPS = 1e-06
 F32 = jnp.float32
 BF16 = jnp.bfloat16
@@ -51,7 +52,16 @@
     sibling = base + chip * 2 + 1 - core
     low, high = chip % 2, chip // 2
     others = [chip + 1 - 2 * low, chip + 2 - 4 * high, 3 - chip]
-    cross = [base + o * 2 + core for o in others]
+    order = [2, core, 1 - core]
+
+    def other(r):
+        if isinstance(r, int):
+            return others[r]
+        return chip + (1 - r) * (1 - 2 * low) + r * (2 - 4 * high)
+
+    def peer(r):
+        return base + other(r) * 2 + core
+
     first = sec == 0
     last = sec == sections - 1
     after = (me + GROUP) % (sections * GROUP)
@@ -65,7 +75,7 @@
         )
 
     loads = [
-        pltpu.make_async_copy(hid, X.at[0, pos], load_sem.at[0]),
+        pltpu.make_async_copy(hid, X.at[0, chip, core], load_sem.at[0]),
         pltpu.make_async_copy(wqkv.at[0], W.at[:, pl.ds(0, width)], load_sem.at[1]),
         pltpu.make_async_copy(wqkv.at[1], W.at[:, pl.ds(width, width)], load_sem.at[2]),
         pltpu.make_async_copy(wqkv.at[2], W.at[:, pl.ds(2 * width, width)], load_sem.at[3]),
@@ -87,8 +97,8 @@
         pl.semaphore_signal(barrier, inc=1, device_id={"section": target}, device_id_type=MESH)
 
     greet(sibling)
-    for target in cross:
-        greet(target)
+    for r in range(CHIPS - 1):
+        greet(peer(r))
 
     @pl.when(first)
     def _():
@@ -151,14 +161,13 @@
 
     def gather(t):
         def forward(c):
-            wait_for(X.at[t, pl.ds(0, 3), :, cols[c]], ag_sem.at[c])
-            for o in others:
-                block = X.at[t, o * 2 + core, :, cols[c]]
-                remote(block, block, send_sem.at[0], agsib_sem.at[c], sibling).start()
+            wait_for(X.at[t, pl.ds(0, CHIPS - 1), 0, :, cols[c]], ag_sem.at[c])
+            blocks = X.at[t, :, core, :, cols[c]]
+            remote(blocks, blocks, send_sem.at[5], agsib_sem.at[c], sibling).start()
 
         def multiply(c, state):
-            wait_for(X.at[t, pl.ds(0, CHIPS), :, cols[c]], agsib_sem.at[c])
-            x = X[t, :, :, cols[c]].reshape(tokens, step).astype(F32)
+            wait_for(X.at[t, :, 0, :, cols[c]], agsib_sem.at[c])
+            x = X[t, :, :, :, cols[c]].reshape(tokens, step).astype(F32)
             if state is None:
                 start = jnp.mean(x, axis=-1, keepdims=True)
             else:
@@ -172,16 +181,16 @@
                 return start, s1, s2, raw
             return start, state[1] + s1, state[2] + s2, state[3] + raw
 
+        state = None
         for c in range(CHUNKS):
 
             @pl.when(t > 0)
             def _():
-                wait_for(X.at[t, pos, :, cols[c]], relay_sem.at[t, c])
-
-            block = X.at[t, pos, :, cols[c]]
-            for target in reversed(cross):
-                remote(block, block, send_sem.at[0], ag_sem.at[c], target).start()
-            remote(block, block, send_sem.at[0], agsib_sem.at[c], sibling).start()
+                wait_for(X.at[t, chip, core, :, cols[c]], relay_sem.at[t, c])
+
+            block = X.at[t, chip, core, :, cols[c]]
+            for r in order:
+                remote(block, block, send_sem.at[0], ag_sem.at[c], peer(r)).start()
             if c == 0:
 
                 @pl.when(t == 0)
@@ -198,7 +207,7 @@
                         load.wait()
 
             if c > 1:
-                state = multiply(c - 2, state if c > 2 else None)
+                state = multiply(c - 2, state)
         state = multiply(CHUNKS - 2, state)
         forward(CHUNKS - 1)
         start, s1, s2, raw = multiply(CHUNKS - 1, state)
@@ -208,7 +217,8 @@
         shift_sums = raw[tokens + 2 : tokens + 3] + raw[tokens + 3 : tokens + 4]
         SW[0:1, :] = shift_sums
         QKV[...] = inverse * (raw[:tokens] - rest * scale_sums) + shift_sums
-        wait_for(X.at[t, pl.ds(0, GROUP - 1)], send_sem.at[0])
+        wait_for(X.at[t, pl.ds(0, CHIPS - 1), 0], send_sem.at[0])
+        wait_for(X.at[t, :, 0], send_sem.at[5])
 
     def fold():
         centre = jnp.mean(WE[...].astype(F32), axis=-1, keepdims=True)
@@ -293,36 +303,37 @@
             both = PF[core, :, :, cols[c]] + RB[par, :, :, cols[c]].astype(F32)
             PF[core, :, :, cols[c]] = both
             CB[:, :, cols[c]] = both.astype(BF16)
-            for r in reversed(range(CHIPS - 1)):
+            for r in order:
                 remote(
-                    CB.at[others[r], :, cols[c]], CR.at[par, r, :, cols[c]],
-                    send_sem.at[2], cross_sem.at[par, c], cross[r],
+                    CB.at[other(r), :, cols[c]], CR.at[par, r, :, cols[c]],
+                    send_sem.at[2], cross_sem.at[par, c], peer(r),
                 ).start()
 
         for c in range(CHUNKS):
             project(c)
-            if c > 0:
-                share(c - 1)
-        share(CHUNKS - 1)
+            if c >= LAG:
+                share(c - LAG)
+        for c in range(CHUNKS - LAG, CHUNKS):
+            share(c)
 
         @pl.when(jnp.logical_and(t > 0, first))
         def _():
             z = Z[t, pos][:, :latents]
             for c in range(CHUNKS):
-                X[t, pos, :, cols[c]] = embed(z, c)
+                X[t, chip, core, :, cols[c]] = embed(z, c)
 
         for c in range(CHUNKS):
             wait_for(CR.at[par, :, :, cols[c]], cross_sem.at[par, c])
             summed = PF[core, chip, :, cols[c]]
             for r in range(CHIPS - 1):
                 summed = summed + CR[par, r, :, cols[c]].astype(F32)
-            result = X[t, pos, :, cols[c]].astype(F32) + param(2, c) * summed
+            result = X[t, chip, core, :, cols[c]].astype(F32) + param(2, c) * summed
             R[:, cols[c]] = result.astype(BF16)
 
             @pl.when(jnp.logical_not(last))
             def _():
                 remote(
-                    R.at[:, cols[c]], X.at[t + 1, pos, :, cols[c]],
+                    R.at[:, cols[c]], X.at[t + 1, chip, core, :, cols[c]],
                     send_sem.at[3], relay_sem.at[t + 1, c], after,
                 ).start()
 
@@ -371,8 +382,8 @@
     def _():
         wait_for(Z.at[ticks, pos], z_sem.at[ticks])
         for c in range(CHUNKS):
-            wait_for(X.at[ticks, pos, :, cols[c]], relay_sem.at[ticks, c])
-        hout[...] = X[ticks, pos]
+            wait_for(X.at[ticks, chip, core, :, cols[c]], relay_sem.at[ticks, c])
+        hout[...] = X[ticks, chip, core]
 
     lout[...] = Z[ticks, pos][:, :latents]
 
@@ -403,7 +414,7 @@
         ],
         out_specs=(vmem, vmem),
         scratch_shapes=[
-            pltpu.VMEM((ticks + 1, GROUP, rows, depth), BF16),
+            pltpu.VMEM((ticks + 1, CHIPS, 2, rows, depth), BF16),
             pltpu.VMEM((ticks + 1, GROUP, rows, lanes), BF16),
             pltpu.VMEM((depth, 3 * width), BF16),
             pltpu.VMEM((width, depth), BF16),
@@ -433,7 +444,7 @@
             dma((CHUNKS,)),
             dma((ticks + 1, CHUNKS)),
             dma((ticks + 1,)),
-            dma((5,)),
+            dma((6,)),
         ],
         compiler_params=pltpu.CompilerParams(
             collective_id=0, has_side_effects=True, vmem_limit_bytes=64 * 1024 * 1024

time: 142 us -> 137 us (0.965)
  Pallas kernels: 138 us -> 134 us
    pallas_call x1, Pallas kernels: 138 us -> 134 us  [body(): pl.pallas_call(functools.partial(kernel, sections), out_shape=(jax.ShapeD...]
where the time goes in v3:
time: 137 us
  Pallas kernels  134 us (98%)
  local copies, waits for them, and re-layouts  2.81 us (2%)
    pallas_call x1, Pallas kernels, body(): pl.pallas_call(functools.partial(kernel, sections), out_shape=(jax.ShapeD...  134 us
    unnamed x2, local copies, waits for them, and re-layouts  2.81 us

profile of v3, /device:TPU:0, one launch (start us, length us, event | category | flops | bytes accessed | tf_op | source)
XLA Modules:
  0.0 137.2 jit_solution(9539523430205356909)
XLA Ops:
  0.6 133.7 %shard_map.122 = (bf16[16,3072]{1,0:T(8,128)(2,1)}, bf16[16,64]{1,0:T(8,128)(2,1)}) custom-call(bf16[16,3072]{1,0:T(8,128)(2,1)} %hid.1, bf16[16,64]{1,0:T(8,128)(2,1)} %lat.1, bf16[3,3072,384]{2,1,0:T(8,128)(2,1)} %wqkv.1, bf16[384,3072]{1,0:T(8,128)(2,1)} %wout.1, bf16[2,256,384]{2,1,0:T(8,128)(2,1)} %kv.1, f32[2,2,128]{2,1,0:T(2,128)} %gain_in.1, ...), custom_call_target="tpu_custom_call" | custom-call | flops 7247757312 | bytes 10000000 | tf_op jit(solution)/shard_map/pallas_call | solution.py:405
  134.3 1.5 %copy.15 = bf16[16,3072]{1,0:T(8,128)(2,1)} copy(bf16[16,3072]{1,0:T(8,128)(2,1)} %get-tuple-element.4) | data formatting | bytes 196608
  135.9 1.3 copy.16

commit v4 on v3

--- a/solution.py
+++ b/solution.py
@@ -11,7 +11,8 @@
 HS = 128
 GROUP = 8
 CHIPS = GROUP // 2
-CHUNKS = 3
+SHARES = (5, 4, 3)
+CHUNKS = len(SHARES)
 EXTRA = 16
 LAG = 2
 EPS = 1e-06
@@ -40,8 +41,9 @@
     total = kv.shape[1]
     tokens = rows * GROUP
     heads = width // HS
-    step = depth // CHUNKS
-    cols = [pl.ds(c * step, step) for c in range(CHUNKS)]
+    unit = depth // sum(SHARES)
+    steps = [share * unit for share in SHARES]
+    cols = [pl.ds(sum(steps[:c]), steps[c]) for c in range(CHUNKS)]
 
     me = lax.axis_index("section")
     sec = me // GROUP
@@ -140,19 +142,43 @@
     def param(k, c):
         return mod[k, pl.ds(sec, 1), cols[c]]
 
+    def extra_rows(scale, shift):
+        row = lax.broadcasted_iota(jnp.int32, (EXTRA, scale.shape[1]), 0)
+        block = jnp.zeros((EXTRA, scale.shape[1]), F32)
+        for k, v in enumerate(split(scale) + split(shift)):
+            block = jnp.where(row == k, v.astype(F32), block)
+        return block.astype(BF16)
+
+    def accumulate(x, scale, extra, times, state):
+        if state is None:
+            start = jnp.mean(x, axis=-1, keepdims=True)
+        else:
+            start = state[0]
+        d = x - start
+        s1 = jnp.sum(d, axis=-1, keepdims=True)
+        s2 = jnp.sum(d * d, axis=-1, keepdims=True)
+        raw = times(jnp.concatenate([(d * scale).astype(BF16), extra], axis=0))
+        if state is None:
+            return start, s1, s2, raw
+        return start, state[1] + s1, state[2] + s2, state[3] + raw
+
+    def finish(state):
+        start, s1, s2, raw = state
+        count = start.shape[0]
+        rest = s1 / depth
+        inverse = lax.rsqrt(jnp.maximum(s2 / depth - rest * rest, 0.0) + EPS)
+        scale_sums = raw[count : count + 1] + raw[count + 1 : count + 2]
+        shift_sums = raw[count + 2 : count + 3] + raw[count + 3 : count + 4]
+        return inverse * (raw[:count] - rest * scale_sums) + shift_sums, shift_sums
+
     def prepare():
         ZS[...] = jnp.zeros_like(ZS)
         Z[0, pos] = jnp.zeros((rows, lanes), BF16)
         loads[11].wait()
         Z[0, pos, :, 0:latents] = LAT[...]
         loads[10].wait()
-        row = lax.broadcasted_iota(jnp.int32, (EXTRA, step), 0)
-        for c in range(CHUNKS):
-            parts = split(1.0 + param(1, c)) + split(param(0, c))
-            block = jnp.zeros((EXTRA, step), F32)
-            for k, v in enumerate(parts):
-                block = jnp.where(row == k, v.astype(F32), block)
-            EX[:, cols[c]] = block.astype(BF16)
+        for c in range(CHUNKS):
+            EX[:, cols[c]] = extra_rows(1.0 + param(1, c), param(0, c))
 
     loads[0].wait()
 
@@ -167,19 +193,12 @@
 
         def multiply(c, state):
             wait_for(X.at[t, :, 0, :, cols[c]], agsib_sem.at[c])
-            x = X[t, :, :, :, cols[c]].reshape(tokens, step).astype(F32)
-            if state is None:
-                start = jnp.mean(x, axis=-1, keepdims=True)
-            else:
-                start = state[0]
-            d = x - start
-            s1 = jnp.sum(d, axis=-1, keepdims=True)
-            s2 = jnp.sum(d * d, axis=-1, keepdims=True)
-            y = jnp.concatenate([(d * (1.0 + param(1, c))).astype(BF16), EX[:, cols[c]]], axis=0)
-            raw = jnp.dot(y, W[cols[c], :], preferred_element_type=F32)
-            if state is None:
-                return start, s1, s2, raw
-            return start, state[1] + s1, state[2] + s2, state[3] + raw
+            x = X[t, :, :, :, cols[c]].reshape(tokens, steps[c]).astype(F32)
+
+            def times(y):
+                return jnp.dot(y, W[cols[c], :], preferred_element_type=F32)
+
+            return accumulate(x, 1.0 + param(1, c), EX[:, cols[c]], times, state)
 
         state = None
         for c in range(CHUNKS):
@@ -210,13 +229,9 @@
                 state = multiply(c - 2, state)
         state = multiply(CHUNKS - 2, state)
         forward(CHUNKS - 1)
-        start, s1, s2, raw = multiply(CHUNKS - 1, state)
-        rest = s1 / depth
-        inverse = lax.rsqrt(jnp.maximum(s2 / depth - rest * rest, 0.0) + EPS)
-        scale_sums = raw[tokens : tokens + 1] + raw[tokens + 1 : tokens + 2]
-        shift_sums = raw[tokens + 2 : tokens + 3] + raw[tokens + 3 : tokens + 4]
+        values, shift_sums = finish(multiply(CHUNKS - 1, state))
         SW[0:1, :] = shift_sums
-        QKV[...] = inverse * (raw[:tokens] - rest * scale_sums) + shift_sums
+        QKV[...] = values
         wait_for(X.at[t, pl.ds(0, CHIPS - 1), 0], send_sem.at[0])
         wait_for(X.at[t, :, 0], send_sem.at[5])
 
@@ -289,7 +304,7 @@
 
         def project(c):
             product = jnp.dot(attended, WO[:, cols[c]], preferred_element_type=F32)
-            product = product.reshape(CHIPS, 2, rows, step)
+            product = product.reshape(CHIPS, 2, rows, steps[c])
             for side in range(2):
                 PF[side, :, :, cols[c]] = product[:, side]
             SB[:, :, cols[c]] = PF[1 - core, :, :, cols[c]].astype(BF16)
@@ -322,39 +337,41 @@
             for c in range(CHUNKS):
                 X[t, chip, core, :, cols[c]] = embed(z, c)
 
-        for c in range(CHUNKS):
+        def combine(c):
             wait_for(CR.at[par, :, :, cols[c]], cross_sem.at[par, c])
             summed = PF[core, chip, :, cols[c]]
             for r in range(CHIPS - 1):
                 summed = summed + CR[par, r, :, cols[c]].astype(F32)
             result = X[t, chip, core, :, cols[c]].astype(F32) + param(2, c) * summed
-            R[:, cols[c]] = result.astype(BF16)
-
-            @pl.when(jnp.logical_not(last))
-            def _():
+            return result.astype(BF16)
+
+        @pl.when(jnp.logical_not(last))
+        def _():
+            copy = remote(Z.at[t, pos], Z.at[t + 1, pos], send_sem.at[4], z_sem.at[t + 1], after)
+            copy.start()
+            for c in range(CHUNKS):
+                R[:, cols[c]] = combine(c)
                 remote(
                     R.at[:, cols[c]], X.at[t + 1, chip, core, :, cols[c]],
                     send_sem.at[3], relay_sem.at[t + 1, c], after,
                 ).start()
-
-        @pl.when(jnp.logical_not(last))
-        def _():
-            copy = remote(Z.at[t, pos], Z.at[t + 1, pos], send_sem.at[4], z_sem.at[t + 1], after)
-            copy.start()
             wait_for(Z.at[t, pos], send_sem.at[4])
             wait_for(R, send_sem.at[3])
 
         @pl.when(last)
         def _():
-            x = R[...].astype(F32)
-            centred = x - jnp.mean(x, axis=-1, keepdims=True)
-            spread = jnp.mean(centred * centred, axis=-1, keepdims=True)
-            normed = (
-                centred * lax.rsqrt(spread + EPS) * (1.0 + fmod[1:2, :]) + fmod[0:1, :]
-            ).astype(BF16)
-            velocity = lax.dot_general(
-                normed, WF[...], (((1,), (1,)), ((), ())), preferred_element_type=F32
-            )
+            state = None
+            for c in range(CHUNKS):
+
+                def times(y):
+                    return lax.dot_general(
+                        y, WF[:, cols[c]], (((1,), (1,)), ((), ())), preferred_element_type=F32
+                    )
+
+                scale = 1.0 + fmod[1:2, cols[c]]
+                extra = extra_rows(scale, fmod[0:1, cols[c]])
+                state = accumulate(combine(c).astype(F32), scale, extra, times, state)
+            velocity, _ = finish(state)
             renewed = (Z[t, pos][:, :latents].astype(F32) + velocity).astype(BF16)
             ZS[...] = jnp.concatenate([renewed, renewed], axis=1)
             for i in range(GROUP):

time: 137 us -> 137 us (level)
  no operation moved by 1% of the time
where the time goes in v4:
time: 137 us
  Pallas kernels  133 us (97%)
  local copies, waits for them, and re-layouts  2.81 us (2%)
    pallas_call x1, Pallas kernels, body(): pl.pallas_call(functools.partial(kernel, sections), out_shape=(jax.ShapeD...  133 us
    unnamed x2, local copies, waits for them, and re-layouts  2.81 us

profile of v4, /device:TPU:0, one launch (start us, length us, event | category | flops | bytes accessed | tf_op | source)
XLA Modules:
  0.0 136.5 jit_solution(9268247116879786682)
XLA Ops:
  0.6 133.0 %shard_map.122 = (bf16[16,3072]{1,0:T(8,128)(2,1)}, bf16[16,64]{1,0:T(8,128)(2,1)}) custom-call(bf16[16,3072]{1,0:T(8,128)(2,1)} %hid.1, bf16[16,64]{1,0:T(8,128)(2,1)} %lat.1, bf16[3,3072,384]{2,1,0:T(8,128)(2,1)} %wqkv.1, bf16[384,3072]{1,0:T(8,128)(2,1)} %wout.1, bf16[2,256,384]{2,1,0:T(8,128)(2,1)} %kv.1, f32[2,2,128]{2,1,0:T(2,128)} %gain_in.1, ...), custom_call_target="tpu_custom_call" | custom-call | flops 7247757312 | bytes 10000000 | tf_op jit(solution)/shard_map/pallas_call | solution.py:422
  133.7 1.5 %copy.15 = bf16[16,3072]{1,0:T(8,128)(2,1)} copy(bf16[16,3072]{1,0:T(8,128)(2,1)} %get-tuple-element.4) | data formatting | bytes 196608
  135.2 1.3 copy.16

commit v5 on v4

--- a/solution.py
+++ b/solution.py
@@ -11,7 +11,7 @@
 HS = 128
 GROUP = 8
 CHIPS = GROUP // 2
-SHARES = (5, 4, 3)
+SHARES = (7, 5)
 CHUNKS = len(SHARES)
 EXTRA = 16
 LAG = 2

time: 137 us -> 139 us (1.015)
  Pallas kernels: 133 us -> 135 us
    pallas_call x1, Pallas kernels: 133 us -> 135 us  [body(): pl.pallas_call(functools.partial(kernel, sections), out_shape=(jax.ShapeD...]
where the time goes in v5:
time: 139 us; the launch traced here: 138 us
  Pallas kernels  135 us (97%)
  local copies, waits for them, and re-layouts  2.81 us (2%)
    pallas_call x1, Pallas kernels, body(): pl.pallas_call(functools.partial(kernel, sections), out_shape=(jax.ShapeD...  135 us
    unnamed x2, local copies, waits for them, and re-layouts  2.81 us

profile of v5, /device:TPU:0, one launch (start us, length us, event | category | flops | bytes accessed | tf_op | source)
XLA Modules:
  0.0 138.4 jit_solution(11847654896561300438)
XLA Ops:
  0.6 135.0 %shard_map.122 = (bf16[16,3072]{1,0:T(8,128)(2,1)}, bf16[16,64]{1,0:T(8,128)(2,1)}) custom-call(bf16[16,3072]{1,0:T(8,128)(2,1)} %hid.1, bf16[16,64]{1,0:T(8,128)(2,1)} %lat.1, bf16[3,3072,384]{2,1,0:T(8,128)(2,1)} %wqkv.1, bf16[384,3072]{1,0:T(8,128)(2,1)} %wout.1, bf16[2,256,384]{2,1,0:T(8,128)(2,1)} %kv.1, f32[2,2,128]{2,1,0:T(2,128)} %gain_in.1, ...), custom_call_target="tpu_custom_call" | custom-call | flops 7247757312 | bytes 10000000 | tf_op jit(solution)/shard_map/pallas_call | solution.py:422
  135.6 1.5 %copy.15 = bf16[16,3072]{1,0:T(8,128)(2,1)} copy(bf16[16,3072]{1,0:T(8,128)(2,1)} %get-tuple-element.4) | data formatting | bytes 196608
  137.1 1.3 copy.16

commit v6 on v4

--- a/solution.py
+++ b/solution.py
@@ -187,9 +187,15 @@
 
     def gather(t):
         def forward(c):
-            wait_for(X.at[t, pl.ds(0, CHIPS - 1), 0, :, cols[c]], ag_sem.at[c])
+            for k in (0, 2):
+                wait_for(X.at[t, 0, 0, :, cols[c]], ag_sem.at[k, c])
             blocks = X.at[t, :, core, :, cols[c]]
             remote(blocks, blocks, send_sem.at[5], agsib_sem.at[c], sibling).start()
+
+        def hand_on(c):
+            wait_for(X.at[t, 0, 0, :, cols[c]], ag_sem.at[1, c])
+            block = X.at[t, other(1), core, :, cols[c]]
+            remote(block, block, send_sem.at[0], ag_sem.at[2, c], peer(0)).start()
 
         def multiply(c, state):
             wait_for(X.at[t, :, 0, :, cols[c]], agsib_sem.at[c])
@@ -208,8 +214,8 @@
                 wait_for(X.at[t, chip, core, :, cols[c]], relay_sem.at[t, c])
 
             block = X.at[t, chip, core, :, cols[c]]
-            for r in order:
-                remote(block, block, send_sem.at[0], ag_sem.at[c], peer(r)).start()
+            for r in (1, 0):
+                remote(block, block, send_sem.at[0], ag_sem.at[r, c], peer(r)).start()
             if c == 0:
 
                 @pl.when(t == 0)
@@ -217,7 +223,7 @@
                     prepare()
 
             if c > 0:
-                forward(c - 1)
+                hand_on(c - 1)
             if c == 1:
 
                 @pl.when(t == 0)
@@ -226,9 +232,13 @@
                         load.wait()
 
             if c > 1:
-                state = multiply(c - 2, state)
+                forward(c - 2)
+        hand_on(CHUNKS - 1)
+        forward(CHUNKS - 2)
+        for c in range(CHUNKS - 2):
+            state = multiply(c, state)
+        forward(CHUNKS - 1)
         state = multiply(CHUNKS - 2, state)
-        forward(CHUNKS - 1)
         values, shift_sums = finish(multiply(CHUNKS - 1, state))
         SW[0:1, :] = shift_sums
         QKV[...] = values
@@ -457,7 +467,7 @@
             dma((12,)),
             dma((2, CHUNKS)),
             dma((2, CHUNKS)),
-            dma((CHUNKS,)),
+            dma((3, CHUNKS)),
             dma((CHUNKS,)),
             dma((ticks + 1, CHUNKS)),
             dma((ticks + 1,)),

time: 137 us -> 145 us (1.058)
  Pallas kernels: 133 us -> 142 us
    pallas_call x1, Pallas kernels: 133 us -> 142 us  [body(): pl.pallas_call(functools.partial(kernel, sections), out_shape=(jax.ShapeD...]
where the time goes in v6:
time: 145 us
  Pallas kernels  142 us (98%)
  local copies, waits for them, and re-layouts  2.81 us (2%)
    pallas_call x1, Pallas kernels, body(): pl.pallas_call(functools.partial(kernel, sections), out_shape=(jax.ShapeD...  142 us

profile of v6, /device:TPU:0, one launch (start us, length us, event | category | flops | bytes accessed | tf_op | source)
XLA Modules:
  0.0 145.2 jit_solution(16647738301462380576)
XLA Ops:
  0.6 141.7 %shard_map.122 = (bf16[16,3072]{1,0:T(8,128)(2,1)}, bf16[16,64]{1,0:T(8,128)(2,1)}) custom-call(bf16[16,3072]{1,0:T(8,128)(2,1)} %hid.1, bf16[16,64]{1,0:T(8,128)(2,1)} %lat.1, bf16[3,3072,384]{2,1,0:T(8,128)(2,1)} %wqkv.1, bf16[384,3072]{1,0:T(8,128)(2,1)} %wout.1, bf16[2,256,384]{2,1,0:T(8,128)(2,1)} %kv.1, f32[2,2,128]{2,1,0:T(2,128)} %gain_in.1, ...), custom_call_target="tpu_custom_call" | custom-call | flops 7247757312 | bytes 10000000 | tf_op jit(solution)/shard_map/pallas_call | solution.py:432
  142.4 1.5 %copy.15 = bf16[16,3072]{1,0:T(8,128)(2,1)} copy(bf16[16,3072]{1,0:T(8,128)(2,1)} %get-tuple-element.4) | data formatting | bytes 196608
  143.9 1.3 copy.16

commit v7 on v4

--- a/solution.py
+++ b/solution.py
@@ -70,6 +70,9 @@
     before = (me + (sections - 1) * GROUP) % (sections * GROUP)
     last_base = (sections - 1) * GROUP
 
+    def facing(r):
+        return base + other(r) * 2 + 1 - core
+
     def remote(src, dst, send, recv, target):
         return pltpu.make_async_remote_copy(
             src_ref=src, dst_ref=dst, send_sem=send, recv_sem=recv,
@@ -101,6 +104,7 @@
     greet(sibling)
     for r in range(CHIPS - 1):
         greet(peer(r))
+        greet(facing(r))
 
     @pl.when(first)
     def _():
@@ -123,17 +127,17 @@
             greet(before)
 
     if sections == 2:
-        pl.semaphore_wait(barrier, CHIPS + GROUP)
+        pl.semaphore_wait(barrier, GROUP - 1 + GROUP)
     else:
         edge = jnp.logical_or(first, last)
 
         @pl.when(edge)
         def _():
-            pl.semaphore_wait(barrier, CHIPS + GROUP + 1)
+            pl.semaphore_wait(barrier, GROUP - 1 + GROUP + 1)
 
         @pl.when(jnp.logical_not(edge))
         def _():
-            pl.semaphore_wait(barrier, CHIPS + 2)
+            pl.semaphore_wait(barrier, GROUP - 1 + 2)
 
     def split(v):
         high_part = v.astype(BF16)
@@ -188,6 +192,8 @@
     def gather(t):
         def forward(c):
             wait_for(X.at[t, pl.ds(0, CHIPS - 1), 0, :, cols[c]], ag_sem.at[c])
+            if c == CHUNKS - 1:
+                return
             blocks = X.at[t, :, core, :, cols[c]]
             remote(blocks, blocks, send_sem.at[5], agsib_sem.at[c], sibling).start()
 
@@ -210,6 +216,10 @@
             block = X.at[t, chip, core, :, cols[c]]
             for r in order:
                 remote(block, block, send_sem.at[0], ag_sem.at[c], peer(r)).start()
+            if c == CHUNKS - 1:
+                for r in order:
+                    remote(block, block, send_sem.at[5], agsib_sem.at[c], facing(r)).start()
+                remote(block, block, send_sem.at[5], agsib_sem.at[c], sibling).start()
             if c == 0:
 
                 @pl.when(t == 0)

time: 137 us -> 133 us (0.971)
  Pallas kernels: 133 us -> 129 us
    pallas_call x1, Pallas kernels: 133 us -> 129 us  [body(): pl.pallas_call(functools.partial(kernel, sections), out_shape=(jax.ShapeD...]
where the time goes in v7:
time: 133 us; the launch traced here: 132 us
  Pallas kernels  129 us (97%)
  local copies, waits for them, and re-layouts  2.81 us (2%)
    pallas_call x1, Pallas kernels, body(): pl.pallas_call(functools.partial(kernel, sections), out_shape=(jax.ShapeD...  129 us
    unnamed x2, local copies, waits for them, and re-layouts  2.81 us

profile of v7, /device:TPU:0, one launch (start us, length us, event | category | flops | bytes accessed | tf_op | source)
XLA Modules:
  0.0 132.5 jit_solution(7147666776500179838)
XLA Ops:
  0.6 129.0 %shard_map.122 = (bf16[16,3072]{1,0:T(8,128)(2,1)}, bf16[16,64]{1,0:T(8,128)(2,1)}) custom-call(bf16[16,3072]{1,0:T(8,128)(2,1)} %hid.1, bf16[16,64]{1,0:T(8,128)(2,1)} %lat.1, bf16[3,3072,384]{2,1,0:T(8,128)(2,1)} %wqkv.1, bf16[384,3072]{1,0:T(8,128)(2,1)} %wout.1, bf16[2,256,384]{2,1,0:T(8,128)(2,1)} %kv.1, f32[2,2,128]{2,1,0:T(2,128)} %gain_in.1, ...), custom_call_target="tpu_custom_call" | custom-call | flops 7247757312 | bytes 10000000 | tf_op jit(solution)/shard_map/pallas_call | solution.py:432
  129.7 1.5 %copy.15 = bf16[16,3072]{1,0:T(8,128)(2,1)} copy(bf16[16,3072]{1,0:T(8,128)(2,1)} %get-tuple-element.4) | data formatting | bytes 196608
  131.2 1.3 copy.16
